TPU v7x, 32 devices: a whole 2x2x4 slice. The times are simulated.
32 devices in a mesh: run: 2 (over core), row: 4 (over y, x), col: 4 (over z).
Axes of the slice: x: 2, y: 2, z: 4, core: 2. Of those that a mesh axis runs over, the one named last changes fastest.
Arguments:
- init_field: float32 [96, 256, 512], P('run', 'row', 'col'), may hold values from -6 to 6
- conduct: float32 [256, 512], P('row', 'col'), may hold values from 0.5 to 2
- nonlin: float32 [96], P('run'), may hold values from 0.1 to 1
- counts: int32 [96], P('run'), may hold values from 1 to 8
- descriptors: bfloat16 [96, 256], replicated, may hold values from -6 to 6
- time_code: bfloat16 [8, 256], replicated, may hold values from -6 to 6
- w_in: bfloat16 [256, 512], replicated, may hold values from -0.375 to 0.375
- bias_in: float32 [512], replicated, may hold values from -6 to 6
- w_out: bfloat16 [512, 512], replicated, may hold values from -0.25 to 0.25
- decoder: bfloat16 [512, 256, 512], P(None, ('row', 'col')), may hold values from -0.22 to 0.22
Outputs:
- final_field: float32 [96, 256, 512], P('run', 'row', 'col')
- new_w_in: float32 [256, 512], replicated
- new_bias: float32 [512], replicated
- new_w_out: float32 [512, 512], replicated
- mean_loss: float32 [], replicated
All inputs are finite; a program needn't handle non-finite values.
Results may differ from a plain program's by a relative error of at most 0.0017.
Values may be sent and summed in bfloat16 or wider, within the bound.
No kernel may reach another device: no remote copies, remote signals or barrier semaphores. Data moves between devices by JAX's collectives and lax.ppermute only.
A program may use at most 128 MiB of HBM per device.

v0:
```python
import functools

import jax
import jax.numpy as jnp
import numpy as np
from jax import lax
from jax.experimental import pallas as pl
from jax.experimental.pallas import tpu as pltpu
from jax.sharding import PartitionSpec as P

time_step = 0.12
learn_rate = 0.5
LANES = 128
SUB = 8
GROUP = 16
f32 = jnp.float32
bf16 = jnp.bfloat16


def neighbours(up, down, axis):
    count = lax.axis_size(axis)
    forward = [(i, i + 1) for i in range(count - 1)]
    backward = [(target, source) for source, target in forward]
    return lax.ppermute(up, axis, forward), lax.ppermute(down, axis, backward)


def kappa_of(u, cond, nonlin):
    divisor = 1.0 + nonlin * (u * u)
    guess = pltpu.reciprocal(divisor, approx=True)
    return cond * (guess * (2.0 - divisor * guess))


def apart(wide):
    parts = wide // LANES
    source = np.arange(wide)[:, None]
    place = np.arange(wide)[None, :]
    return jnp.asarray(source == parts * (place % LANES) + place // LANES, bf16)


def decoder_kernel(d_ref, order_ref, out_ref, wide_ref):
    size, band, wide = d_ref.shape
    x = d_ref[...]
    if band % 16:
        x = x.astype(f32).reshape(size * band, wide).astype(bf16)
    else:
        x = x.reshape(size * band, wide)
    y = jnp.dot(x, order_ref[...], preferred_element_type=f32)
    for part in range(wide // LANES):
        wide_ref[part] = y[:, part * LANES : (part + 1) * LANES]
    for row in range(band):
        for part in range(wide // LANES):
            lanes = pl.ds(row * wide + part * LANES, LANES)
            out_ref[:, lanes] = wide_ref[part, pl.ds(row, size, stride=band), :].astype(bf16)


ROW_SEGS = 8
COL_SEGS = 16


def tile_order(halo, cols_dev):
    across = (cols_dev + 2 * halo) // COL_SEGS
    lanes = ROW_SEGS * COL_SEGS
    place = np.arange(across * lanes)
    column = (place % COL_SEGS) * across + place // lanes
    seg_row = (place % lanes) // COL_SEGS
    source = np.arange(ROW_SEGS * cols_dev)[:, None]
    main = (source // cols_dev == seg_row) & (source % cols_dev + halo == column)
    half = ROW_SEGS * halo
    parity = np.arange(2)[:, None, None, None]
    high = np.arange(2)[:, None, None]
    source = np.arange(LANES)[:, None]
    edge = (
        (source // half == parity)
        & (source % half // halo == seg_row)
        & (source % halo + high * (cols_dev + halo) == column)
    )
    return jnp.asarray(main, bf16), jnp.asarray(edge.reshape(2, 2 * LANES, -1), bf16)


def row_source(halo, rows_dev, runs, refs):
    x_ref, cond_ref, top_ref, bottom_ref = refs

    def source(row):
        if row < halo:
            return top_ref[pl.ds(row, runs, stride=halo), :], top_ref[pl.ds(runs * halo + row, 1), :]
        row -= halo
        if row < rows_dev:
            return x_ref[pl.ds(row, runs, stride=rows_dev), :], cond_ref[pl.ds(row, 1), :]
        row -= rows_dev
        return (
            bottom_ref[pl.ds(row, runs, stride=halo), :],
            bottom_ref[pl.ds(runs * halo + row, 1), :],
        )

    def both(row, copies):
        runs_of, cond = source(row)
        return jnp.concatenate([runs_of, jnp.broadcast_to(cond, (copies, LANES))], axis=0)

    return both


def pack_kernel(halo, runs, x_ref, cond_ref, top_ref, bottom_ref, low_ref, high_ref):
    rows_dev = cond_ref.shape[0]
    source = row_source(halo, rows_dev, runs, (x_ref, cond_ref, top_ref, bottom_ref))
    deep = (rows_dev + 2 * halo) // ROW_SEGS
    half = ROW_SEGS * halo
    lane = lax.broadcasted_iota(jnp.int32, (runs + SUB, LANES), 1)
    for block in range(low_ref.shape[0]):
        low = jnp.zeros((runs + SUB, LANES), f32)
        high = jnp.zeros((runs + SUB, LANES), f32)
        for parity in range(2):
            if 2 * block + parity >= deep:
                break
            for seg in range(ROW_SEGS):
                value = source(seg * deep + 2 * block + parity, SUB)
                spot = parity * half + seg * halo
                here = (lane >= spot) & (lane < spot + halo)
                first = pltpu.roll(value, spot, 1) if spot else value
                shift = (spot + halo) % LANES
                last = pltpu.roll(value, shift, 1) if shift else value
                low = jnp.where(here, first, low)
                high = jnp.where(here, last, high)
        low_ref[block] = low
        high_ref[block] = high


PIECES = 3


def pieces_of(x):
    high = x.astype(bf16)
    rest = x - high.astype(f32)
    middle = rest.astype(bf16)
    return high, middle, (rest - middle.astype(f32)).astype(bf16)


def tile_kernel(
    halo, steps, runs, x_ref, cond_ref, top_ref, bottom_ref, left_ref, right_ref, nonlin_ref,
    counts_ref, main_ref, edge_ref, out_ref, u_ref, c_ref, rate_ref, body_ref, ends_ref, back_ref,
):
    rows_dev, cols_dev = cond_ref.shape
    source = row_source(halo, rows_dev, runs, (x_ref, cond_ref, top_ref, bottom_ref))
    deep = (rows_dev + 2 * halo) // ROW_SEGS
    across = (cols_dev + 2 * halo) // COL_SEGS
    tall = runs + GROUP
    row_at, row_count = lax.axis_index("row"), lax.axis_size("row")
    col_at, col_count = lax.axis_index("col"), lax.axis_size("col")

    for b in range(deep):
        for seg in range(ROW_SEGS):
            for i, piece in enumerate(pieces_of(source(seg * deep + b, GROUP))):
                body_ref[i, b * tall : (b + 1) * tall, seg * cols_dev : (seg + 1) * cols_dev] = piece
        for side, ref in enumerate((left_ref, right_ref)):
            value = jnp.concatenate([ref[b // 2], ref[b // 2, runs:]], axis=0)
            for i, piece in enumerate(pieces_of(value)):
                first = b // 2 * tall
                ends_ref[i, b % 2, first : first + tall, side * LANES : (side + 1) * LANES] = piece

    lane = lax.broadcasted_iota(jnp.int32, (SUB, LANES), 1)
    chunk = 3 if across % 3 == 0 else 1
    for start in range(0, across, chunk):
        lanes = slice(start * LANES, (start + chunk) * LANES)
        total = None
        for i in range(PIECES):
            part = jnp.dot(body_ref[i], main_ref[:, lanes], preferred_element_type=f32)
            total = part if total is None else total + part
        extra = []
        for parity in range(2):
            more = None
            for i in range(PIECES):
                part = jnp.dot(
                    ends_ref[i, parity], edge_ref[parity, :, lanes], preferred_element_type=f32
                )
                more = part if more is None else more + part
            extra.append(more)
        for b in range(deep):
            first = b // 2 * tall
            value = total[b * tall : (b + 1) * tall] + extra[b % 2][first : first + tall]
            for inner in range(chunk):
                q = start + inner
                here = value[:, inner * LANES : (inner + 1) * LANES]
                u_ref[0, b, q] = here[:runs]
                c_ref[b + 1, q] = here[runs : runs + SUB]
    for b in range(deep):
        for q in range(across):
            row = lane // COL_SEGS * deep + b
            col = lane % COL_SEGS * across + q
            inside = (
                ((row >= halo) | (row_at > 0))
                & ((row < halo + rows_dev) | (row_at < row_count - 1))
                & ((col >= halo) | (col_at > 0))
                & ((col < halo + cols_dev) | (col_at < col_count - 1))
            )
            rate_ref[b, q] = jnp.where(inside, 0.5 * time_step, 0.0)
    for q in range(across):
        c_ref[0, q] = pltpu.roll(c_ref[deep, q], COL_SEGS, 1)
        c_ref[deep + 1, q] = pltpu.roll(c_ref[1, q], LANES - COL_SEGS, 1)

    def group(index, _):
        where = pl.ds(pl.multiple_of(index * SUB, SUB), SUB)
        nonlin = nonlin_ref[where, :]
        counts = counts_ref[where, :]

        def step(number, old, new):
            active = jnp.where(number < counts, 1.0, 0.0)

            def get(b, q):
                if b < 0:
                    u = pltpu.roll(u_ref[old, deep - 1, q, where, :], COL_SEGS, 1)
                elif b == deep:
                    u = pltpu.roll(u_ref[old, 0, q, where, :], LANES - COL_SEGS, 1)
                else:
                    u = u_ref[old, b, q, where, :]
                return u, kappa_of(u, c_ref[b + 1, q], nonlin)

            last = [get(-1, q) for q in range(across)]
            here = [get(0, q) for q in range(across)]
            below = [(k0 + k1) * (u1 - u0) for (u0, k0), (u1, k1) in zip(last, here)]
            for b in range(deep):
                u = [pair[0] for pair in here]
                k = [pair[1] for pair in here]
                u.append(pltpu.roll(u[0], LANES - 1, 1))
                k.append(pltpu.roll(k[0], LANES - 1, 1))
                side = [(k[q] + k[q + 1]) * (u[q + 1] - u[q]) for q in range(across)]
                side.append(pltpu.roll(side[across - 1], 1, 1))
                then = [get(b + 1, q) for q in range(across)]
                above = [(k[q] + then[q][1]) * (then[q][0] - u[q]) for q in range(across)]
                for q in range(across):
                    flux = (above[q] - below[q]) + (side[q] - side[q - 1])
                    u_ref[new, b, q, where, :] = u[q] + (rate_ref[b, q] * active) * flux
                here, below = then, above

        def two(i, _):
            step(2 * i, 0, 1)
            step(2 * i + 1, 1, 0)
            return 0

        lax.fori_loop(0, steps // 2, two, 0)
        return 0

    lax.fori_loop(0, runs // SUB, group, 0)

    for b in range(deep):
        for q in range(across):
            for i, piece in enumerate(pieces_of(u_ref[0, b, q])):
                back_ref[i, b * runs : (b + 1) * runs, q * LANES : (q + 1) * LANES] = piece
    chunk = 2 if ROW_SEGS % 2 == 0 else 1
    for start in range(0, ROW_SEGS, chunk):
        places = slice(start * cols_dev, (start + chunk) * cols_dev)
        total = None
        for i in range(PIECES):
            part = lax.dot_general(
                back_ref[i], main_ref[places, :], (((1,), (1,)), ((), ())), preferred_element_type=f32
            )
            total = part if total is None else total + part
        for b in range(deep):
            for inner in range(chunk):
                row = (start + inner) * deep + b - halo
                if 0 <= row < rows_dev:
                    out_ref[pl.ds(row, runs, stride=rows_dev), :] = total[
                        b * runs : (b + 1) * runs, inner * cols_dev : (inner + 1) * cols_dev
                    ]


def strip_kernel(halo, steps, runs, *refs):
    count = lax.axis_size("col")
    blocks = refs[:count]
    order_ref, nonlin_ref, counts_ref = refs[count : count + 3]
    out_ref, square_ref, u_ref, c_ref, turned_ref, wide_ref = refs[count + 4 :]
    cols_dev = blocks[0].shape[2]
    wide = count * cols_dev
    parts = wide // LANES
    rows = u_ref.shape[0]
    band = rows - 2 * halo
    index = pl.program_id(0)
    col_at = lax.axis_index("col")
    row_at, row_count = lax.axis_index("row"), lax.axis_size("row")
    has_top = (row_at > 0) | (col_at > 0)
    has_bottom = (row_at < row_count - 1) | (col_at < count - 1)
    lane = lax.broadcasted_iota(jnp.int32, (GROUP, LANES), 1)
    first_lane, last_lane = lane == 0, lane == LANES - 1

    def ordered(get):
        whole = jnp.concatenate([get(block) for block in blocks], axis=1)
        return jnp.dot(whole, turned_ref[...], preferred_element_type=f32)

    @pl.when(index == 0)
    def _():
        for back in range(count):
            at = lax.rem(col_at + count - back, count)
            turned_ref[back * cols_dev : (back + 1) * cols_dev, :] = order_ref[
                pl.ds(pl.multiple_of(at * cols_dev, cols_dev), cols_dev), :
            ]
        plane = ordered(lambda block: block[runs])
        for row in range(rows):
            c_ref[row] = jnp.broadcast_to(plane[row : row + 1], (SUB, wide))
        square_ref[...] = jnp.zeros_like(square_ref)

    def split(x):
        return [x[..., part * LANES : (part + 1) * LANES] for part in range(parts)]

    where = pl.ds(pl.multiple_of(index * GROUP, GROUP), GROUP)
    fields = ordered(lambda block: block[where].reshape(GROUP * rows, cols_dev))
    for part, values in enumerate(split(fields)):
        wide_ref[part] = values
    for row in range(rows):
        for part in range(parts):
            lanes = pl.ds(part * LANES, LANES)
            u_ref[row, :, lanes] = wide_ref[part, pl.ds(row, GROUP, stride=rows), :]
    nonlin = nonlin_ref[where, :]
    counts = counts_ref[where, :]

    def get(row):
        u = split(u_ref[row])
        cond = split(jnp.concatenate([c_ref[row]] * (GROUP // SUB), axis=0))
        return u, [kappa_of(a, b, nonlin) for a, b in zip(u, cond)]

    for number in range(steps):
        factor = jnp.where(number < counts, 0.5 * time_step, 0.0)
        top_scale = jnp.where(has_top, factor, 0.0)
        bottom_scale = jnp.where(has_bottom, factor, 0.0)

        def one(row, carry, scale, keep):
            u, k, below, square = carry
            then_u, then_k = get(row + 1)
            above = [(a + b) * (c - d) for a, b, c, d in zip(k, then_k, then_u, u)]
            u_more = u + [jnp.where(last_lane, 0.0, pltpu.roll(u[0], LANES - 1, 1))]
            k_more = k + [jnp.where(last_lane, 0.0, pltpu.roll(k[0], LANES - 1, 1))]
            side = [(k_more[p] + k_more[p + 1]) * (u_more[p + 1] - u_more[p]) for p in range(parts)]
            start = jnp.where(first_lane, k[0] * u[0], pltpu.roll(side[-1], 1, 1))
            side = [start] + side
            for p in range(parts):
                fresh = u[p] + scale * ((above[p] - below[p]) + (side[p + 1] - side[p]))
                u_ref[row, :, pl.ds(p * LANES, LANES)] = fresh
                if keep:
                    shot = fresh.astype(bf16)
                    lanes = pl.ds((row - halo) * wide + p * LANES, LANES)
                    out_ref[0, pl.ds(number * GROUP, GROUP), lanes] = shot
                    again = shot.astype(f32)
                    square = square + again * again
            return then_u, then_k, above, square

        last_u, last_k = get(number)
        u, k = get(number + 1)
        below = [(a + b) * (c - d) for a, b, c, d in zip(k, last_k, u, last_u)]
        carry = (u, k, below, jnp.zeros((GROUP, LANES), f32))
        for row in range(number + 1, halo):
            carry = one(row, carry, top_scale, False)
        for row in range(halo, halo + band):
            carry = one(row, carry, factor, True)
        for row in range(halo + band, rows - 1 - number):
            carry = one(row, carry, bottom_scale, False)
        square_ref[...] += carry[3]


def share_kernel(scale_of, pieces_ref, loss_ref, out_ref):
    total = pieces_ref[0].astype(f32)
    for source in range(1, pieces_ref.shape[0]):
        total = total + pieces_ref[source].astype(f32)
    rows = [piece.astype(f32) for piece in pieces_of(loss_ref[...])]
    filler = jnp.zeros((out_ref.shape[1] - total.shape[0] - PIECES, total.shape[1]), f32)
    message = jnp.concatenate([total] + rows + [filler], axis=0).astype(bf16)
    for target in range(out_ref.shape[0]):
        out_ref[target] = message


def finish_kernel(
    share, loss_scale, mine_ref, other_ref, act_ref, slope_ref, rows_ref, w_in_ref, bias_ref,
    w_out_ref, new_in_ref, new_bias_ref, new_out_ref, loss_ref, grad_ref, parts_ref,
):
    core = lax.axis_index("run")
    cells = mine_ref.shape[0]
    for at, ref in ((core, mine_ref), (1 - core, other_ref)):
        parts = jnp.zeros((1, ref.shape[2]), f32)
        rows = []
        for source in range(cells):
            value = ref[source].astype(f32)
            rows.append(value[:share])
            for piece in range(PIECES):
                parts = parts + value[share + piece : share + piece + 1]
        size = cells * share
        grad_ref[pl.ds(pl.multiple_of(at * size, size), size), :] = jnp.concatenate(
            rows, axis=0
        ).astype(bf16)
        parts_ref[pl.ds(at, 1), :] = parts
    loss = jnp.sum(parts_ref[0:1] + parts_ref[1:2], axis=1, keepdims=True) * loss_scale
    loss_ref[...] = jnp.broadcast_to(loss, loss_ref.shape)
    grad = grad_ref[...]
    by_rows = (((0,), (0,)), ((), ()))
    grad_out = lax.dot_general(act_ref[...], grad, by_rows, preferred_element_type=f32)
    new_out_ref[...] = w_out_ref[...].astype(f32) - learn_rate * grad_out
    back = lax.dot_general(
        grad, w_out_ref[...], (((1,), (1,)), ((), ())), preferred_element_type=f32
    )
    grad_pre = back * slope_ref[...]
    new_bias_ref[...] = bias_ref[...] - learn_rate * jnp.sum(grad_pre, axis=0, keepdims=True)
    grad_in = lax.dot_general(
        rows_ref[...], grad_pre.astype(bf16), by_rows, preferred_element_type=f32
    )
    new_in_ref[...] = w_in_ref[...].astype(f32) - learn_rate * grad_in


def per_device(
    init_field, conduct, nonlin, counts, descriptors, time_code, w_in, bias_in, w_out, decoder
):
    runs, rows_dev, cols_dev = init_field.shape
    steps = time_code.shape[0]
    inputs, hidden_size = w_in.shape
    run_size = lax.axis_size("run")
    row_size = lax.axis_size("row")
    col_size = lax.axis_size("col")
    halo = steps
    band = rows_dev // col_size
    rows_strip = band + 2 * halo
    wide = cols_dev * col_size
    groups = runs // GROUP
    runs_total = runs * run_size
    rows_all = runs_total * steps
    scale_of = 1.0 / rows_all
    vmem = pltpu.CompilerParams(vmem_limit_bytes=56 * 1024 * 1024)
    in_vmem = pl.BlockSpec(memory_space=pltpu.VMEM)
    anywhere = pl.BlockSpec(memory_space=pl.ANY)

    tile = jnp.concatenate([init_field, conduct[None]], axis=0)
    top, bottom = neighbours(tile[:, rows_dev - halo :], tile[:, :halo], "row")

    padded = jnp.concatenate([top, tile, bottom], axis=1).astype(bf16)
    col_at = lax.axis_index("col")

    def message(target):
        return lax.dynamic_slice_in_dim(padded, target * band, rows_strip, 1)

    messages = [message((col_at + hop) % col_size) for hop in range(col_size)]

    deep = (rows_dev + 2 * halo) // ROW_SEGS
    across = (cols_dev + 2 * halo) // COL_SEGS
    tall = runs + GROUP
    tile_args = (
        init_field.reshape(runs * rows_dev, cols_dev),
        conduct,
        top.reshape(-1, cols_dev),
        bottom.reshape(-1, cols_dev),
    )
    pack_shape = jax.ShapeDtypeStruct((-(-deep // 2), runs + SUB, LANES), f32)
    low, high = pl.pallas_call(
        functools.partial(pack_kernel, halo, runs),
        out_shape=(pack_shape, pack_shape),
        in_specs=[in_vmem] * 4,
        out_specs=(in_vmem, in_vmem),
        compiler_params=vmem,
        name="pack_columns",
    )(*tile_args)
    (low, high, decoder), messages = lax.optimization_barrier(((low, high, decoder), messages))
    left, right = neighbours(high, low, "col")
    blocks = messages[:1]
    for hop in range(1, col_size):
        pairs = [(i, (i + hop) % col_size) for i in range(col_size)]
        blocks.append(lax.ppermute(messages[hop], "col", pairs))

    nonlin_wide = jnp.broadcast_to(nonlin[:, None], (runs, LANES))
    counts_wide = jnp.broadcast_to(counts[:, None], (runs, LANES))
    field = pl.pallas_call(
        functools.partial(tile_kernel, halo, steps, runs),
        out_shape=jax.ShapeDtypeStruct((runs * rows_dev, cols_dev), f32),
        in_specs=[in_vmem] * 10,
        out_specs=in_vmem,
        scratch_shapes=[
            pltpu.VMEM((2, deep, across, runs, LANES), f32),
            pltpu.VMEM((deep + 2, across, SUB, LANES), f32),
            pltpu.VMEM((deep, across, SUB, LANES), f32),
            pltpu.VMEM((PIECES, deep * tall, ROW_SEGS * cols_dev), bf16),
            pltpu.VMEM((PIECES, 2, -(-deep // 2) * tall, 2 * LANES), bf16),
            pltpu.VMEM((PIECES, deep * runs, across * LANES), bf16),
        ],
        compiler_params=vmem,
        name="tile_solver",
    )(*tile_args, left, right, nonlin_wide, counts_wide, *tile_order(halo, cols_dev))
    final_field = field.reshape(init_field.shape)

    desc = descriptors.astype(f32).reshape(run_size * groups, 1, GROUP, -1)
    codes = time_code.astype(f32)[None, :, None, :]
    rows_in = (desc + codes).astype(bf16).reshape(rows_all, -1)
    pre = jnp.dot(rows_in, w_in, preferred_element_type=f32) + bias_in
    act, pull = jax.vjp(jax.nn.gelu, pre)
    slope = pull(jnp.ones_like(pre))[0]
    act = act.astype(bf16)
    hidden = jnp.dot(act, w_out, preferred_element_type=f32).astype(bf16)
    hidden, slope = lax.optimization_barrier((hidden, slope))
    mine = lax.dynamic_slice_in_dim(hidden, lax.axis_index("run") * runs * steps, runs * steps, 0)

    order = apart(wide)
    size = 64
    weights = pl.pallas_call(
        decoder_kernel,
        grid=(hidden_size // size,),
        out_shape=jax.ShapeDtypeStruct((hidden_size, band * wide), bf16),
        in_specs=[
            pl.BlockSpec((size, band, wide), lambda i: (i, 0, 0)),
            pl.BlockSpec((wide, wide), lambda i: (0, 0)),
        ],
        out_specs=pl.BlockSpec((size, band * wide), lambda i: (i, 0)),
        scratch_shapes=[pltpu.VMEM((wide // LANES, size * band, LANES), f32)],
        compiler_params=vmem,
        name="decoder_order",
    )(decoder, order)
    last_dims = (((1,), (1,)), ((), ()))
    gram = lax.dot_general(weights, weights, last_dims, preferred_element_type=f32)
    pushed = None
    rest = gram
    for _ in range(PIECES):
        piece = lax.reduce_precision(rest, 8, 7)
        rest = rest - piece
        part = jnp.dot(mine, piece.astype(bf16), preferred_element_type=f32)
        pushed = part if pushed is None else pushed + part

    shots, squares = pl.pallas_call(
        functools.partial(strip_kernel, halo, steps, runs),
        grid=(groups,),
        out_shape=(
            jax.ShapeDtypeStruct((groups, GROUP * steps, band * wide), bf16),
            jax.ShapeDtypeStruct((GROUP, LANES), f32),
        ),
        in_specs=[in_vmem] * (col_size + 3) + [anywhere],
        out_specs=(
            pl.BlockSpec((1, GROUP * steps, band * wide), lambda i: (i, 0, 0)),
            pl.BlockSpec((GROUP, LANES), lambda i: (0, 0)),
        ),
        scratch_shapes=[
            pltpu.VMEM((rows_strip, GROUP, wide), f32),
            pltpu.VMEM((rows_strip, SUB, wide), f32),
            pltpu.VMEM((wide, wide), bf16),
            pltpu.VMEM((wide // LANES, GROUP * rows_strip, LANES), f32),
        ],
        compiler_params=vmem,
        name="strip_solver",
    )(*blocks, order, nonlin_wide, counts_wide, field)

    drawn = lax.dot_general(
        shots.reshape(runs * steps, band * wide), weights, last_dims, preferred_element_type=f32
    )
    partial = ((pushed - drawn) * scale_of).astype(bf16)
    loss = jnp.sum(mine.astype(f32) * (pushed - 2.0 * drawn), axis=0, keepdims=True)
    loss = loss + jnp.pad(jnp.sum(squares, axis=0, keepdims=True), ((0, 0), (0, hidden_size - LANES)))

    cells = row_size * col_size
    share = runs * steps // cells
    pieces = lax.all_to_all(
        partial.reshape(cells, share, hidden_size), ("row", "col"), 0, 0, tiled=True
    )
    taller = -(-(share + PIECES) // 16) * 16
    message_out = pl.pallas_call(
        functools.partial(share_kernel, scale_of),
        out_shape=jax.ShapeDtypeStruct((cells, taller, hidden_size), bf16),
        in_specs=[in_vmem] * 2,
        out_specs=in_vmem,
        compiler_params=vmem,
        name="share_sum",
    )(pieces, loss)
    gathered = lax.all_to_all(message_out, ("row", "col"), 0, 0, tiled=True)
    swap = [(i, (i + 1) % run_size) for i in range(run_size)]
    other = lax.ppermute(gathered, "run", swap)
    cells_total = rows_dev * row_size * wide
    new_w_in, new_bias, new_w_out, mean_loss = pl.pallas_call(
        functools.partial(finish_kernel, share, 1.0 / (rows_all * cells_total)),
        out_shape=(
            jax.ShapeDtypeStruct((inputs, hidden_size), f32),
            jax.ShapeDtypeStruct((1, hidden_size), f32),
            jax.ShapeDtypeStruct((hidden_size, hidden_size), f32),
            jax.ShapeDtypeStruct((1, LANES), f32),
        ),
        in_specs=[in_vmem] * 8,
        out_specs=(in_vmem,) * 4,
        scratch_shapes=[
            pltpu.VMEM((rows_all, hidden_size), bf16),
            pltpu.VMEM((run_size, hidden_size), f32),
        ],
        compiler_params=vmem,
        name="trunk_update",
    )(gathered, other, act, slope, rows_in, w_in, bias_in[None], w_out)
    return (final_field, new_w_in, new_bias[0], new_w_out, mean_loss[0, 0])


def solution(mesh):
    in_specs = (
        P("run", "row", "col"),
        P("row", "col"),
        P("run"),
        P("run"),
        P(),
        P(),
        P(),
        P(),
        P(),
        P(None, ("row", "col"), None),
    )
    out_specs = (P("run", "row", "col"), P(), P(), P(), P())
    return jax.shard_map(
        per_device, mesh=mesh, in_specs=in_specs, out_specs=out_specs, check_vma=False
    )
```

profile of v0, /device:TPU:0, one launch (start us, length us, event | category | flops | bytes accessed | tf_op | source)
XLA Modules:
  0.0 169.0 jit_solution(7246501242638650798)
XLA Ops:
  0.6 0.0 copy-start.18
  0.6 0.0 copy-start.16
  0.7 0.0 copy-start.19
  0.7 0.0 copy-start.13
  0.7 1.8 %fusion.15 = (f32[49,8,128]{2,1,0:T(8,128)}, f32[49,8,128]{2,1,0:T(8,128)}) fusion(f32[48,64,128]{2,1,0:T(8,128)} %param.13, f32[1,64,128]{2,1,0:T(8,128)} %bitcast.33), kind=kLoop, calls=%fused_computation.34 | loop fusion | flops 100352 | bytes 2007040 | tf_op jit(solution)/shard_map/concatenate | solution.py:424
  2.5 1.3 collective-permute-start.1
  3.8 5.5 %collective-permute-start = (f32[49,8,128]{2,1,0:T(8,128)}, f32[49,8,128]{2,1,0:T(8,128)S(1)}, u32[]{:S(2)}, u32[]{:S(2)}) collective-permute-start(f32[49,8,128]{2,1,0:T(8,128)} %get-tuple-element.40), channel_id=1, source_target_pairs={{0,4},{4,8},{8,12},{1,5},{5,9},{9,13},{2,6},{6,10},{10,14},{3,7},{... | collective-permute-start | bytes 602120 | tf_op jit(solution)/shard_map/ppermute | solution.py:24
  9.3 0.1 add_convert_fusion
  9.5 0.0 copy-start.8
  9.5 2.4 %fusion.6 = (f32[768,512]{1,0:T(8,128)}, bf16[768,512]{1,0:T(8,128)(2,1)S(1)}) fusion(f32[512]{0:T(512)S(1)} %copy-done.19, bf16[768,256]{1,0:T(8,128)(2,1)S(1)} %bitcast.31, bf16[256,512]{1,0:T(8,128)(2,1)S(1)} %copy-done.13), kind=kOutput, calls=%fused_computation.11 | convolution fusion | flops 209190912 | bytes 3016704 | tf_op jit(solution)/shard_map/dot_general | solution.py:483
  11.9 0.9 copy-done.6
  12.8 0.6 convolution_convert_fusion
  13.4 0.2 copy-done
  13.6 0.1 fusion
  13.7 0.0 collective-permute-done.1
  13.7 0.1 collective-permute-done
  13.8 0.5 copy-done.2
  14.4 0.2 copy-done.3
  14.5 3.6 %pack_columns.1 = (f32[5,56,128]{2,1,0:T(8,128)}, f32[5,56,128]{2,1,0:T(8,128)}) custom-call(f32[3072,128]{1,0:T(8,128)} %bitcast.24, f32[64,128]{1,0:T(8,128)} %cond_ref.3, f32[392,128]{1,0:T(8,128)} %bitcast.29, f32[392,128]{1,0:T(8,128)} %bitcast.27), custom_call_target="tpu_custom_call" | custom-call | tf_op jit(solution)/shard_map/pack_columns/pallas_call | solution.py:445
  18.1 0.9 convert.12
  19.0 0.9 convert.10
  20.0 0.1 pad_maximum_fusion.1
  20.1 0.0 copy-start.23
  20.1 0.0 copy-start.22
  20.1 1.1 constant_dynamic-slice_fusion
  21.1 0.0 copy-done.23
  21.1 3.9 %collective-permute-start.2 = (f32[5,56,128]{2,1,0:T(8,128)S(1)}, f32[5,56,128]{2,1,0:T(8,128)S(1)}, u32[]{:S(2)}, u32[]{:S(2)}) collective-permute-start(f32[5,56,128]{2,1,0:T(8,128)S(1)} %copy-done.23), channel_id=1, source_target_pairs={{0,1},{1,2},{2,3},{4,5},{5,6},{6,7},{8,9},{9,10},{10,11},{12,13},{... | collective-permute-start | bytes 430088 | tf_op jit(solution)/shard_map/ppermute | solution.py:24
  25.1 0.0 copy-done.22
  25.1 1.3 collective-permute-start.3
  26.4 2.7 %collective-permute-start.4 = (bf16[49,32,128]{2,1,0:T(8,128)(2,1)S(1)}, bf16[49,32,128]{2,1,0:T(8,128)(2,1)S(1)}, u32[]{:S(2)}, u32[]{:S(2)}) collective-permute-start(bf16[49,32,128]{2,1,0:T(8,128)(2,1)S(1)} %get-tuple-element.29), channel_id=1, source_target_pairs={{0,1},{1,2},{2,3},{3,0},{4,5},{5,6},{6,7},{7,4},{8,9},{9,10},{10,1... | collective-permute-start | bytes 1204232 | tf_op jit(solution)/shard_map/ppermute | solution.py:458
  29.1 2.6 %collective-permute-start.5 = (bf16[49,32,128]{2,1,0:T(8,128)(2,1)S(1)}, bf16[49,32,128]{2,1,0:T(8,128)(2,1)S(1)}, u32[]{:S(2)}, u32[]{:S(2)}) collective-permute-start(bf16[49,32,128]{2,1,0:T(8,128)(2,1)S(1)} %get-tuple-element.30), channel_id=1, source_target_pairs={{0,2},{1,3},{2,0},{3,1},{4,6},{5,7},{6,4},{7,5},{8,10},{9,11},{10,... | collective-permute-start | bytes 1204232 | tf_op jit(solution)/shard_map/ppermute | solution.py:458
  31.6 1.3 collective-permute-start.6
  33.0 14.4 %decoder_order.1 = bf16[512,8192]{1,0:T(8,128)(2,1)} custom-call(bf16[512,16,512]{2,1,0:T(8,128)(2,1)} %d_ref, bf16[512,512]{1,0:T(8,128)(2,1)} %constant.78.clone.order_ref.refs_4_), custom_call_target="tpu_custom_call" | custom-call | tf_op jit(solution)/shard_map/decoder_order/pallas_call | solution.py:493
  47.4 10.5 %fusion.19 = f32[512,512]{1,0:T(8,128)S(1)} fusion(bf16[512,8192]{1,0:T(8,128)(2,1)} %decoder_order.1), kind=kOutput, calls=%fused_computation.43 | convolution fusion | flops 4294967296 | bytes 9437184 | tf_op jit(solution)/shard_map/dot_general | solution.py:507
  57.9 0.4 fusion.10
  58.2 0.4 convolution_add_fusion.2
  58.6 0.0 copy-start.20
  58.6 0.0 copy-start.21
  58.7 0.4 convolution_add_fusion.1
  59.1 0.0 collective-permute-done.2.left_ref
  59.1 0.0 copy-start.14
  59.1 0.0 collective-permute-done.3.right_ref
  59.1 0.2 copy-done.20
  59.3 0.7 broadcast_in_dim.13.nonlin_ref.refs_5_
  60.0 0.7 broadcast_in_dim.28.counts_ref.refs_6_
  60.6 31.8 %tile_solver.1.refs_7_ = f32[3072,128]{1,0:T(8,128)} custom-call(f32[3072,128]{1,0:T(8,128)} %bitcast.25, f32[64,128]{1,0:T(8,128)} %cond_ref.3, f32[392,128]{1,0:T(8,128)} %bitcast.30, f32[392,128]{1,0:T(8,128)} %bitcast.28, f32[5,56,128]{2,1,0:T(8,128)} %copy-done.14, f32[5,56,128]{2,1,0:T(8,128)} %copy-done.15, ...), custom_call_target="tpu_custom_call" | custom-call | tf_op jit(solution)/shard_map/tile_solver/pallas_call | solution.py:462
  92.5 0.0 collective-permute-done.4.refs_1_
  92.5 0.0 collective-permute-done.5.refs_2_
  92.5 0.0 collective-permute-done.6.refs_3_
  92.5 0.7 copy-done.10
  93.2 0.1 copy-done.11
  93.4 0.8 copy-done.12
  94.1 19.9 %strip_solver.1 = (bf16[3,128,8192]{2,1,0:T(8,128)(2,1)}, f32[16,128]{1,0:T(8,128)}) custom-call(bf16[49,32,128]{2,1,0:T(8,128)(2,1)} %get-tuple-element.28.refs_0_, bf16[49,32,128]{2,1,0:T(8,128)(2,1)} %copy-done.10, bf16[49,32,128]{2,1,0:T(8,128)(2,1)} %copy-done.11, bf16[49,32,128]{2,1,0:T(8,128)(2,1)} %copy-done.12, ...), custom_call_target="tpu_custom_call" | custom-call | tf_op jit(solution)/shard_map/strip_solver/pallas_call | solution.py:516
  114.0 9.5 %multiply_reduce_fusion = (f32[512]{0:T(512)S(1)}, bf16[384,512]{1,0:T(8,128)(2,1)}) fusion(f32[384,512]{1,0:T(8,128)S(1)} %convolution_add_fusion.1, bf16[768,512]{1,0:T(8,128)(2,1)S(1)} %convolution_convert_fusion, s32[]{:T(128)S(6)} %select_n.42, bf16[384,8192]{1,0:T(8,128)(2,1)} %bitcast.39, bf16[512,8192]{1,0:T(8,128)(2,1)} %decoder_order.1), kind=kOutput, calls=%fused_computation.26 | convolution fusion | flops 3222797824 | bytes 16254980 | tf_op jit(solution)/shard_map/dot_general | solution.py:538
  123.5 6.7 %all-to-all-start = ((bf16[16,24,512]{2,1,0:T(8,128)(2,1)}), bf16[16,24,512]{2,1,0:T(8,128)(2,1)S(1)}, u32[]{:S(2)}, u32[]{:S(2)}) async-start(bf16[16,24,512]{2,1,0:T(8,128)(2,1)} %bitcast.8), calls=%async_computation | async-start | bytes 786432 | tf_op jit(solution)/shard_map/all_to_all | solution.py:547
  130.2 0.6 pad_add_fusion.loss_ref
  130.8 10.5 %all-to-all-done.pieces_ref = bf16[16,24,512]{2,1,0:T(8,128)(2,1)S(1)} async-done(((bf16[16,24,512]{2,1,0:T(8,128)(2,1)}), bf16[16,24,512]{2,1,0:T(8,128)(2,1)S(1)}, u32[]{:S(2)}, u32[]{:S(2)}) %all-to-all-start) | async-done | bytes 393248 | tf_op jit(solution)/shard_map/all_to_all | solution.py:547
  141.3 0.7 copy-done.5
  142.1 1.9 %share_sum.1 = bf16[16,32,512]{2,1,0:T(8,128)(2,1)} custom-call(bf16[16,24,512]{2,1,0:T(8,128)(2,1)} %copy-done.5, f32[1,512]{1,0:T(1,128)} %pad_add_fusion.loss_ref), custom_call_target="tpu_custom_call" | custom-call | tf_op jit(solution)/shard_map/share_sum/pallas_call | solution.py:551
  143.9 17.8 %all_to_all.10.mine_ref = bf16[16,32,512]{2,1,0:T(8,128)(2,1)S(1)} all-to-all(bf16[16,32,512]{2,1,0:T(8,128)(2,1)} %share_sum.1), channel_id=1, replica_groups=mesh['run'=2,'row'=4,'col'=4] {'row','col'}, dimensions={0} | all-to-all | bytes 1048576 | tf_op jit(solution)/shard_map/all_to_all | solution.py:559
  161.7 0.0 collective-permute-start.7
  161.7 1.9 %collective-permute-done.7.other_ref = bf16[16,32,512]{2,1,0:T(8,128)(2,1)S(1)} collective-permute-done((bf16[16,32,512]{2,1,0:T(8,128)(2,1)S(1)}, bf16[16,32,512]{2,1,0:T(8,128)(2,1)S(1)}, u32[]{:S(2)}, u32[]{:S(2)}) %collective-permute-start.7) | collective-permute-done | bytes 524320 | tf_op jit(solution)/shard_map/ppermute | solution.py:561
  163.6 0.8 copy-done.9
  164.4 4.6 %trunk_update.1 = (f32[256,512]{1,0:T(8,128)}, f32[1,512]{1,0:T(1,128)}, f32[512,512]{1,0:T(8,128)}, f32[1,128]{1,0:T(1,128)}) custom-call(bf16[16,32,512]{2,1,0:T(8,128)(2,1)} %copy-done.1, bf16[16,32,512]{2,1,0:T(8,128)(2,1)} %copy-done.9, bf16[768,512]{1,0:T(8,128)(2,1)} %copy-done.6, f32[768,512]{1,0:T(8,128)} %get-tuple-element.34.slope_ref, ...), custom_call_target="tpu_custom_call" | custom-call | tf_op jit(solution)/shard_map/trunk_update/pallas_call | solution.py:563
  (29 shorter events, 0.1 us)
Async XLA Ops:
  0.6 8.7 %copy-start.18 = (bf16[8,256]{1,0:T(8,128)(2,1)S(1)}, bf16[8,256]{1,0:T(8,128)(2,1)}, u32[]{:S(2)}) copy-start(bf16[8,256]{1,0:T(8,128)(2,1)} %param.18) | copy-start | bytes 12292
  0.6 8.7 %copy-start.16 = (bf16[96,256]{1,0:T(8,128)(2,1)S(1)}, bf16[96,256]{1,0:T(8,128)(2,1)}, u32[]{:S(2)}) copy-start(bf16[96,256]{1,0:T(8,128)(2,1)} %param.17) | copy-start | bytes 147460
  0.7 8.8 %copy-start.19 = (f32[512]{0:T(512)S(1)}, f32[512]{0:T(512)}, u32[]{:S(2)}) copy-start(f32[512]{0:T(512)} %param.20) | copy-start | bytes 6148
  0.7 8.8 %copy-start.13 = (bf16[256,512]{1,0:T(8,128)(2,1)S(1)}, bf16[256,512]{1,0:T(8,128)(2,1)}, u32[]{:S(2)}) copy-start(bf16[256,512]{1,0:T(8,128)(2,1)} %w_in_ref.1) | copy-start | bytes 786436
  2.5 11.1 %collective-permute-start.1 = (f32[49,8,128]{2,1,0:T(8,128)}, f32[49,8,128]{2,1,0:T(8,128)S(1)}, u32[]{:S(2)}, u32[]{:S(2)}) collective-permute-start(f32[49,8,128]{2,1,0:T(8,128)} %get-tuple-element.39), channel_id=1, source_target_pairs={{4,0},{8,4},{12,8},{5,1},{9,5},{13,9},{6,2},{10,6},{14,10},{7,3},{... | collective-permute-start | bytes 602120 | tf_op jit(solution)/shard_map/ppermute | solution.py:24
  3.8 10.0 %collective-permute-start = (f32[49,8,128]{2,1,0:T(8,128)}, f32[49,8,128]{2,1,0:T(8,128)S(1)}, u32[]{:S(2)}, u32[]{:S(2)}) collective-permute-start(f32[49,8,128]{2,1,0:T(8,128)} %get-tuple-element.40), channel_id=1, source_target_pairs={{0,4},{4,8},{8,12},{1,5},{5,9},{9,13},{2,6},{6,10},{10,14},{3,7},{... | collective-permute-start | bytes 602120 | tf_op jit(solution)/shard_map/ppermute | solution.py:24
  9.4 2.4 %copy-start.4 = (bf16[6,8,16,256]{3,2,1,0:T(8,128)(2,1)}, bf16[6,8,16,256]{3,2,1,0:T(8,128)(2,1)S(1)}, u32[]{:S(2)}) copy-start(bf16[6,8,16,256]{3,2,1,0:T(8,128)(2,1)S(1)} %add_convert_fusion) | copy-start | bytes 1179652
  9.5 3.3 %copy-start.8 = (bf16[512,512]{1,0:T(8,128)(2,1)S(1)}, bf16[512,512]{1,0:T(8,128)(2,1)}, u32[]{:S(2)}) copy-start(bf16[512,512]{1,0:T(8,128)(2,1)} %w_out_ref.1) | copy-start | bytes 1572868
  11.9 0.9 copy-start.6
  11.9 1.7 %copy-start = (f32[48,64,128]{2,1,0:T(8,128)S(1)}, f32[48,64,128]{2,1,0:T(8,128)}, u32[]{:S(2)}) copy-start(f32[48,64,128]{2,1,0:T(8,128)} %param.13) | copy-start | bytes 4718596
  11.9 1.7 %copy-start.7 = (f32[64,128]{1,0:T(8,128)S(1)}, f32[64,128]{1,0:T(8,128)}, u32[]{:S(2)}) copy-start(f32[64,128]{1,0:T(8,128)} %cond_ref.3) | copy-start | bytes 98308
  13.7 0.7 copy-start.2
  13.8 0.7 copy-start.3
  20.1 1.1 copy-start.23
  20.1 5.0 %copy-start.22 = (f32[5,56,128]{2,1,0:T(8,128)S(1)}, f32[5,56,128]{2,1,0:T(8,128)}, u32[]{:S(2)}) copy-start(f32[5,56,128]{2,1,0:T(8,128)} %get-tuple-element.25) | copy-start | bytes 430084
  21.1 38.0 %collective-permute-start.2 = (f32[5,56,128]{2,1,0:T(8,128)S(1)}, f32[5,56,128]{2,1,0:T(8,128)S(1)}, u32[]{:S(2)}, u32[]{:S(2)}) collective-permute-start(f32[5,56,128]{2,1,0:T(8,128)S(1)} %copy-done.23), channel_id=1, source_target_pairs={{0,1},{1,2},{2,3},{4,5},{5,6},{6,7},{8,9},{9,10},{10,11},{12,13},{... | collective-permute-start | bytes 430088 | tf_op jit(solution)/shard_map/ppermute | solution.py:24
  25.1 34.1 %collective-permute-start.3 = (f32[5,56,128]{2,1,0:T(8,128)S(1)}, f32[5,56,128]{2,1,0:T(8,128)S(1)}, u32[]{:S(2)}, u32[]{:S(2)}) collective-permute-start(f32[5,56,128]{2,1,0:T(8,128)S(1)} %copy-done.22), channel_id=1, source_target_pairs={{1,0},{2,1},{3,2},{5,4},{6,5},{7,6},{9,8},{10,9},{11,10},{13,12},{... | collective-permute-start | bytes 430088 | tf_op jit(solution)/shard_map/ppermute | solution.py:24
  26.4 66.1 %collective-permute-start.4 = (bf16[49,32,128]{2,1,0:T(8,128)(2,1)S(1)}, bf16[49,32,128]{2,1,0:T(8,128)(2,1)S(1)}, u32[]{:S(2)}, u32[]{:S(2)}) collective-permute-start(bf16[49,32,128]{2,1,0:T(8,128)(2,1)S(1)} %get-tuple-element.29), channel_id=1, source_target_pairs={{0,1},{1,2},{2,3},{3,0},{4,5},{5,6},{6,7},{7,4},{8,9},{9,10},{10,1... | collective-permute-start | bytes 1204232 | tf_op jit(solution)/shard_map/ppermute | solution.py:458
  29.1 63.4 %collective-permute-start.5 = (bf16[49,32,128]{2,1,0:T(8,128)(2,1)S(1)}, bf16[49,32,128]{2,1,0:T(8,128)(2,1)S(1)}, u32[]{:S(2)}, u32[]{:S(2)}) collective-permute-start(bf16[49,32,128]{2,1,0:T(8,128)(2,1)S(1)} %get-tuple-element.30), channel_id=1, source_target_pairs={{0,2},{1,3},{2,0},{3,1},{4,6},{5,7},{6,4},{7,5},{8,10},{9,11},{10,... | collective-permute-start | bytes 1204232 | tf_op jit(solution)/shard_map/ppermute | solution.py:458
  31.6 60.9 %collective-permute-start.6 = (bf16[49,32,128]{2,1,0:T(8,128)(2,1)S(1)}, bf16[49,32,128]{2,1,0:T(8,128)(2,1)S(1)}, u32[]{:S(2)}, u32[]{:S(2)}) collective-permute-start(bf16[49,32,128]{2,1,0:T(8,128)(2,1)S(1)} %get-tuple-element.31), channel_id=1, source_target_pairs={{0,3},{1,0},{2,1},{3,2},{4,7},{5,4},{6,5},{7,6},{8,11},{9,8},{10,9... | collective-permute-start | bytes 1204232 | tf_op jit(solution)/shard_map/ppermute | solution.py:458
  58.6 0.7 copy-start.20
  58.6 1.3 copy-start.21
  59.1 1.5 copy-start.14
  59.3 1.4 copy-start.15
  92.5 0.7 copy-start.10
  92.5 0.9 copy-start.11
  93.3 0.8 copy-start.12
  114.0 16.2 %copy-start.17 = (f32[16,128]{1,0:T(8,128)S(1)}, f32[16,128]{1,0:T(8,128)}, u32[]{:S(2)}) copy-start(f32[16,128]{1,0:T(8,128)} %get-tuple-element.33) | copy-start | bytes 24580
  123.5 17.9 %all-to-all-start = ((bf16[16,24,512]{2,1,0:T(8,128)(2,1)}), bf16[16,24,512]{2,1,0:T(8,128)(2,1)S(1)}, u32[]{:S(2)}, u32[]{:S(2)}) async-start(bf16[16,24,512]{2,1,0:T(8,128)(2,1)} %bitcast.8), calls=%async_computation | async-start | bytes 786432 | tf_op jit(solution)/shard_map/all_to_all | solution.py:547
  141.3 0.7 copy-start.5
  161.7 1.9 %copy-start.1 = (bf16[16,32,512]{2,1,0:T(8,128)(2,1)}, bf16[16,32,512]{2,1,0:T(8,128)(2,1)S(1)}, u32[]{:S(2)}) copy-start(bf16[16,32,512]{2,1,0:T(8,128)(2,1)S(1)} %all_to_all.10.mine_ref) | copy-start | bytes 1572868
  161.7 1.9 %collective-permute-start.7 = (bf16[16,32,512]{2,1,0:T(8,128)(2,1)S(1)}, bf16[16,32,512]{2,1,0:T(8,128)(2,1)S(1)}, u32[]{:S(2)}, u32[]{:S(2)}) collective-permute-start(bf16[16,32,512]{2,1,0:T(8,128)(2,1)S(1)} %all_to_all.10.mine_ref), channel_id=1, source_target_pairs={{0,16},{16,0},{1,17},{17,1},{2,18},{18,2},{3,19},{19,3},{4,20},{20... | collective-permute-start | bytes 1572872 | tf_op jit(solution)/shard_map/ppermute | solution.py:561
  163.6 0.8 copy-start.9
where the time goes:
time: 170 us; the launch traced here: 169 us
  Pallas kernels  76.1 us (45%)
  starting transfers between devices  25.3 us (15%)
  matrix products  24.1 us (14%)
  blocking collectives  17.8 us (10%)
  waiting for transfers between devices  12.6 us (7%)
  local copies, waits for them, and re-layouts  7.54 us (4%)
  other arithmetic  4.6 us (3%)
    pallas_call x1, Pallas kernels, per_device(): pl.pallas_call(functools.partial(tile_kernel, halo, steps, runs), out_sha...  31.8 us
    pallas_call x1, Pallas kernels, per_device(): pl.pallas_call(functools.partial(strip_kernel, halo, steps, runs), grid=(...  19.9 us
    all_to_all x1, blocking collectives, per_device(): gathered = lax.all_to_all(message_out, ('row', 'col'), 0, 0, tiled=True)  17.8 us
    pallas_call x1, Pallas kernels, per_device(): pl.pallas_call(decoder_kernel, grid=(hidden_size // size,), out_shape=jax...  14.4 us
    ppermute x4, starting transfers between devices, neighbours(): return (lax.ppermute(up, axis, forward), lax.ppermute(down, axis, backward))  12 us
    all_to_all x1, waiting for transfers between devices, per_device(): lax.all_to_all(partial.reshape(cells, share, hidden_size), ('row', 'col')...  10.5 us
    dot_general x1, matrix products, per_device(): lax.dot_general(weights, weights, last_dims, preferred_element_type=f32)  10.5 us
    dot_general x1, matrix products, per_device(): lax.dot_general(shots.reshape(runs * steps, band * wide), weights, last_d...  9.49 us
  transfers between devices with their start and end apart: 9, of which 3 were waited for; matrix products, arithmetic and copies ran while one was open for 10% of the time, Pallas kernels for 27%

commit v1 on v0

--- a/solution.py
+++ b/solution.py
@@ -24,10 +24,8 @@
     return lax.ppermute(up, axis, forward), lax.ppermute(down, axis, backward)
 
 
-def kappa_of(u, cond, nonlin):
-    divisor = 1.0 + nonlin * (u * u)
-    guess = pltpu.reciprocal(divisor, approx=True)
-    return cond * (guess * (2.0 - divisor * guess))
+def kappa_of(u, cond, inverse):
+    return cond * pltpu.reciprocal(inverse + u * u, approx=True)
 
 
 def apart(wide):
@@ -37,9 +35,10 @@
     return jnp.asarray(source == parts * (place % LANES) + place // LANES, bf16)
 
 
-def decoder_kernel(d_ref, order_ref, out_ref, wide_ref):
-    size, band, wide = d_ref.shape
-    x = d_ref[...]
+def reorder(index, size, d_ref, order_ref, out_ref, wide_ref):
+    _, band, wide = d_ref.shape
+    here = pl.ds(pl.multiple_of(index * size, size), size)
+    x = d_ref[here]
     if band % 16:
         x = x.astype(f32).reshape(size * band, wide).astype(bf16)
     else:
@@ -50,7 +49,22 @@
     for row in range(band):
         for part in range(wide // LANES):
             lanes = pl.ds(row * wide + part * LANES, LANES)
-            out_ref[:, lanes] = wide_ref[part, pl.ds(row, size, stride=band), :].astype(bf16)
+            out_ref[here, lanes] = wide_ref[part, pl.ds(row, size, stride=band), :].astype(bf16)
+
+
+def product(left_ref, right_ref):
+    cells = left_ref.shape[1]
+    size = min(cells, 2048)
+    total = None
+    for start in range(0, cells, size):
+        part = lax.dot_general(
+            left_ref[:, start : start + size],
+            right_ref[:, start : start + size],
+            (((1,), (1,)), ((), ())),
+            preferred_element_type=f32,
+        )
+        total = part if total is None else total + part
+    return total
 
 
 ROW_SEGS = 8
@@ -124,20 +138,25 @@
         high_ref[block] = high
 
 
-PIECES = 3
-
-
-def pieces_of(x):
-    high = x.astype(bf16)
-    rest = x - high.astype(f32)
-    middle = rest.astype(bf16)
-    return high, middle, (rest - middle.astype(f32)).astype(bf16)
+LOSS_PIECES = 3
+PIECES = 2
+
+
+def pieces_of(x, count=PIECES):
+    pieces = []
+    for _ in range(count):
+        pieces.append(x.astype(bf16))
+        x = x - pieces[-1].astype(f32)
+    return pieces
 
 
 def tile_kernel(
-    halo, steps, runs, x_ref, cond_ref, top_ref, bottom_ref, left_ref, right_ref, nonlin_ref,
-    counts_ref, main_ref, edge_ref, out_ref, u_ref, c_ref, rate_ref, body_ref, ends_ref, back_ref,
+    halo, steps, runs, x_ref, cond_ref, top_ref, bottom_ref, left_ref, right_ref, inverse_ref,
+    counts_ref, main_ref, edge_ref, order_ref, decoder_hbm, out_ref, weights_hbm, u_ref, c_ref,
+    rate_ref, body_ref, ends_ref, back_ref, decoder_ref, weights_ref, part_ref, sems,
 ):
+    fetch = pltpu.make_async_copy(decoder_hbm, decoder_ref, sems.at[0])
+    fetch.start()
     rows_dev, cols_dev = cond_ref.shape
     source = row_source(halo, rows_dev, runs, (x_ref, cond_ref, top_ref, bottom_ref))
     deep = (rows_dev + 2 * halo) // ROW_SEGS
@@ -196,13 +215,18 @@
         c_ref[0, q] = pltpu.roll(c_ref[deep, q], COL_SEGS, 1)
         c_ref[deep + 1, q] = pltpu.roll(c_ref[1, q], LANES - COL_SEGS, 1)
 
+    size = part_ref.shape[1] // decoder_ref.shape[1]
+    chunks = decoder_ref.shape[0] // size
+    each = -(-chunks // (runs // SUB))
+    fetch.wait()
+
     def group(index, _):
         where = pl.ds(pl.multiple_of(index * SUB, SUB), SUB)
-        nonlin = nonlin_ref[where, :]
+        inverse = inverse_ref[where, :]
         counts = counts_ref[where, :]
 
         def step(number, old, new):
-            active = jnp.where(number < counts, 1.0, 0.0)
+            active = jnp.where(number < counts, inverse, 0.0)
 
             def get(b, q):
                 if b < 0:
@@ -211,7 +235,7 @@
                     u = pltpu.roll(u_ref[old, 0, q, where, :], LANES - COL_SEGS, 1)
                 else:
                     u = u_ref[old, b, q, where, :]
-                return u, kappa_of(u, c_ref[b + 1, q], nonlin)
+                return u, kappa_of(u, c_ref[b + 1, q], inverse)
 
             last = [get(-1, q) for q in range(across)]
             here = [get(0, q) for q in range(across)]
@@ -230,19 +254,22 @@
                     u_ref[new, b, q, where, :] = u[q] + (rate_ref[b, q] * active) * flux
                 here, below = then, above
 
-        def two(i, _):
-            step(2 * i, 0, 1)
-            step(2 * i + 1, 1, 0)
-            return 0
-
-        lax.fori_loop(0, steps // 2, two, 0)
+        done = 0
+        for number in range(steps):
+            step(number, number % 2, 1 - number % 2)
+            while done < each * (number + 1) // steps:
+                chunk = jnp.minimum(index * each + done, chunks - 1)
+                reorder(chunk, size, decoder_ref, order_ref, weights_ref, part_ref)
+                done += 1
         return 0
 
     lax.fori_loop(0, runs // SUB, group, 0)
+    store = pltpu.make_async_copy(weights_ref, weights_hbm, sems.at[1])
+    store.start()
 
     for b in range(deep):
         for q in range(across):
-            for i, piece in enumerate(pieces_of(u_ref[0, b, q])):
+            for i, piece in enumerate(pieces_of(u_ref[steps % 2, b, q])):
                 back_ref[i, b * runs : (b + 1) * runs, q * LANES : (q + 1) * LANES] = piece
     chunk = 2 if ROW_SEGS % 2 == 0 else 1
     for start in range(0, ROW_SEGS, chunk):
@@ -260,13 +287,15 @@
                     out_ref[pl.ds(row, runs, stride=rows_dev), :] = total[
                         b * runs : (b + 1) * runs, inner * cols_dev : (inner + 1) * cols_dev
                     ]
-
-
-def strip_kernel(halo, steps, runs, *refs):
+    store.wait()
+
+
+def strip_kernel(halo, steps, runs, scale_of, *refs):
     count = lax.axis_size("col")
     blocks = refs[:count]
-    order_ref, nonlin_ref, counts_ref = refs[count : count + 3]
-    out_ref, square_ref, u_ref, c_ref, turned_ref, wide_ref = refs[count + 4 :]
+    order_ref, inverse_ref, counts_ref, hidden_ref, weights_hbm = refs[count : count + 5]
+    out_ref, loss_ref, u_ref, c_ref, turned_ref, wide_ref = refs[count + 6 : count + 12]
+    shot_ref, weights_ref, gram_ref, square_ref, sems = refs[count + 12 :]
     cols_dev = blocks[0].shape[2]
     wide = count * cols_dev
     parts = wide // LANES
@@ -284,8 +313,26 @@
         whole = jnp.concatenate([get(block) for block in blocks], axis=1)
         return jnp.dot(whole, turned_ref[...], preferred_element_type=f32)
 
+    groups = runs // GROUP
+    each = -(-band // groups)
+    cells = band * wide
+    fetches = []
+    for part in range(groups):
+        lanes = slice(min(part * each * wide, cells), min((part + 1) * each * wide, cells))
+        if lanes.start < lanes.stop:
+            fetches.append(
+                pltpu.make_async_copy(
+                    weights_hbm.at[:, lanes], weights_ref.at[:, lanes], sems.at[part]
+                )
+            )
+
     @pl.when(index == 0)
     def _():
+        for fetch in fetches:
+            fetch.start()
+        if weights_ref.shape[1] > cells:
+            weights_ref[:, cells:] = jnp.zeros_like(weights_ref[:, cells:])
+        gram_ref[...] = jnp.zeros_like(gram_ref)
         for back in range(count):
             at = lax.rem(col_at + count - back, count)
             turned_ref[back * cols_dev : (back + 1) * cols_dev, :] = order_ref[
@@ -296,6 +343,9 @@
             c_ref[row] = jnp.broadcast_to(plane[row : row + 1], (SUB, wide))
         square_ref[...] = jnp.zeros_like(square_ref)
 
+    for part, fetch in enumerate(fetches):
+        pl.when(index == part)(fetch.wait)
+
     def split(x):
         return [x[..., part * LANES : (part + 1) * LANES] for part in range(parts)]
 
@@ -307,16 +357,17 @@
         for part in range(parts):
             lanes = pl.ds(part * LANES, LANES)
             u_ref[row, :, lanes] = wide_ref[part, pl.ds(row, GROUP, stride=rows), :]
-    nonlin = nonlin_ref[where, :]
+    inverse = inverse_ref[where, :]
     counts = counts_ref[where, :]
+    first_row = pl.multiple_of(index * GROUP * steps, GROUP)
 
     def get(row):
         u = split(u_ref[row])
         cond = split(jnp.concatenate([c_ref[row]] * (GROUP // SUB), axis=0))
-        return u, [kappa_of(a, b, nonlin) for a, b in zip(u, cond)]
+        return u, [kappa_of(a, b, inverse) for a, b in zip(u, cond)]
 
     for number in range(steps):
-        factor = jnp.where(number < counts, 0.5 * time_step, 0.0)
+        factor = jnp.where(number < counts, 0.5 * time_step * inverse, 0.0)
         top_scale = jnp.where(has_top, factor, 0.0)
         bottom_scale = jnp.where(has_bottom, factor, 0.0)
 
@@ -335,7 +386,7 @@
                 if keep:
                     shot = fresh.astype(bf16)
                     lanes = pl.ds((row - halo) * wide + p * LANES, LANES)
-                    out_ref[0, pl.ds(number * GROUP, GROUP), lanes] = shot
+                    shot_ref[pl.ds(first_row + number * GROUP, GROUP), lanes] = shot
                     again = shot.astype(f32)
                     square = square + again * again
             return then_u, then_k, above, square
@@ -351,14 +402,32 @@
         for row in range(halo + band, rows - 1 - number):
             carry = one(row, carry, bottom_scale, False)
         square_ref[...] += carry[3]
-
-
-def share_kernel(scale_of, pieces_ref, loss_ref, out_ref):
+        for spare in range(each * number // steps, each * (number + 1) // steps):
+            lanes = pl.ds(pl.multiple_of((index * each + spare) * wide, wide), wide)
+            cell = weights_ref[:, lanes]
+            gram_ref[...] += lax.dot_general(
+                cell, cell, (((1,), (1,)), ((), ())), preferred_element_type=f32
+            )
+
+    @pl.when(index == pl.num_programs(0) - 1)
+    def _():
+        pushed = None
+        for piece in pieces_of(gram_ref[...]):
+            part = jnp.dot(hidden_ref[...], piece, preferred_element_type=f32)
+            pushed = part if pushed is None else pushed + part
+        drawn = product(shot_ref, weights_ref)
+        out_ref[...] = ((pushed - drawn) * scale_of).astype(bf16)
+        loss = jnp.sum(hidden_ref[...].astype(f32) * (pushed - 2.0 * drawn), axis=0, keepdims=True)
+        loss_ref[...] = loss
+        loss_ref[:, :LANES] += jnp.sum(square_ref[...], axis=0, keepdims=True)
+
+
+def share_kernel(pieces_ref, loss_ref, out_ref):
     total = pieces_ref[0].astype(f32)
     for source in range(1, pieces_ref.shape[0]):
         total = total + pieces_ref[source].astype(f32)
-    rows = [piece.astype(f32) for piece in pieces_of(loss_ref[...])]
-    filler = jnp.zeros((out_ref.shape[1] - total.shape[0] - PIECES, total.shape[1]), f32)
+    rows = [piece.astype(f32) for piece in pieces_of(loss_ref[...], LOSS_PIECES)]
+    filler = jnp.zeros((out_ref.shape[1] - total.shape[0] - LOSS_PIECES, total.shape[1]), f32)
     message = jnp.concatenate([total] + rows + [filler], axis=0).astype(bf16)
     for target in range(out_ref.shape[0]):
         out_ref[target] = message
@@ -376,7 +445,7 @@
         for source in range(cells):
             value = ref[source].astype(f32)
             rows.append(value[:share])
-            for piece in range(PIECES):
+            for piece in range(LOSS_PIECES):
                 parts = parts + value[share + piece : share + piece + 1]
         size = cells * share
         grad_ref[pl.ds(pl.multiple_of(at * size, size), size), :] = jnp.concatenate(
@@ -417,7 +486,10 @@
     runs_total = runs * run_size
     rows_all = runs_total * steps
     scale_of = 1.0 / rows_all
-    vmem = pltpu.CompilerParams(vmem_limit_bytes=56 * 1024 * 1024)
+
+    def vmem(mib):
+        return pltpu.CompilerParams(vmem_limit_bytes=mib * 1024 * 1024)
+
     in_vmem = pl.BlockSpec(memory_space=pltpu.VMEM)
     anywhere = pl.BlockSpec(memory_space=pl.ANY)
 
@@ -447,23 +519,27 @@
         out_shape=(pack_shape, pack_shape),
         in_specs=[in_vmem] * 4,
         out_specs=(in_vmem, in_vmem),
-        compiler_params=vmem,
+        compiler_params=vmem(8),
         name="pack_columns",
     )(*tile_args)
-    (low, high, decoder), messages = lax.optimization_barrier(((low, high, decoder), messages))
+    (low, high), messages = lax.optimization_barrier(((low, high), messages))
     left, right = neighbours(high, low, "col")
     blocks = messages[:1]
     for hop in range(1, col_size):
         pairs = [(i, (i + hop) % col_size) for i in range(col_size)]
         blocks.append(lax.ppermute(messages[hop], "col", pairs))
 
-    nonlin_wide = jnp.broadcast_to(nonlin[:, None], (runs, LANES))
+    inverse_wide = jnp.broadcast_to(1.0 / nonlin[:, None], (runs, LANES))
     counts_wide = jnp.broadcast_to(counts[:, None], (runs, LANES))
-    field = pl.pallas_call(
+    order = apart(wide)
+    field, weights = pl.pallas_call(
         functools.partial(tile_kernel, halo, steps, runs),
-        out_shape=jax.ShapeDtypeStruct((runs * rows_dev, cols_dev), f32),
-        in_specs=[in_vmem] * 10,
-        out_specs=in_vmem,
+        out_shape=(
+            jax.ShapeDtypeStruct((runs * rows_dev, cols_dev), f32),
+            jax.ShapeDtypeStruct((hidden_size, band * wide), bf16),
+        ),
+        in_specs=[in_vmem] * 11 + [anywhere],
+        out_specs=(in_vmem, anywhere),
         scratch_shapes=[
             pltpu.VMEM((2, deep, across, runs, LANES), f32),
             pltpu.VMEM((deep + 2, across, SUB, LANES), f32),
@@ -471,10 +547,15 @@
             pltpu.VMEM((PIECES, deep * tall, ROW_SEGS * cols_dev), bf16),
             pltpu.VMEM((PIECES, 2, -(-deep // 2) * tall, 2 * LANES), bf16),
             pltpu.VMEM((PIECES, deep * runs, across * LANES), bf16),
+            pltpu.VMEM(decoder.shape, bf16),
+            pltpu.VMEM((hidden_size, band * wide), bf16),
+            pltpu.VMEM((wide // LANES, 32 * band, LANES), f32),
+            pltpu.SemaphoreType.DMA((2,)),
         ],
-        compiler_params=vmem,
+        compiler_params=vmem(48),
+        cost_estimate=pl.CostEstimate(flops=10**11, bytes_accessed=10**7, transcendentals=0),
         name="tile_solver",
-    )(*tile_args, left, right, nonlin_wide, counts_wide, *tile_order(halo, cols_dev))
+    )(*tile_args, left, right, inverse_wide, counts_wide, *tile_order(halo, cols_dev), order, decoder)
     final_field = field.reshape(init_field.shape)
 
     desc = descriptors.astype(f32).reshape(run_size * groups, 1, GROUP, -1)
@@ -488,72 +569,42 @@
     hidden, slope = lax.optimization_barrier((hidden, slope))
     mine = lax.dynamic_slice_in_dim(hidden, lax.axis_index("run") * runs * steps, runs * steps, 0)
 
-    order = apart(wide)
-    size = 64
-    weights = pl.pallas_call(
-        decoder_kernel,
-        grid=(hidden_size // size,),
-        out_shape=jax.ShapeDtypeStruct((hidden_size, band * wide), bf16),
-        in_specs=[
-            pl.BlockSpec((size, band, wide), lambda i: (i, 0, 0)),
-            pl.BlockSpec((wide, wide), lambda i: (0, 0)),
-        ],
-        out_specs=pl.BlockSpec((size, band * wide), lambda i: (i, 0)),
-        scratch_shapes=[pltpu.VMEM((wide // LANES, size * band, LANES), f32)],
-        compiler_params=vmem,
-        name="decoder_order",
-    )(decoder, order)
-    last_dims = (((1,), (1,)), ((), ()))
-    gram = lax.dot_general(weights, weights, last_dims, preferred_element_type=f32)
-    pushed = None
-    rest = gram
-    for _ in range(PIECES):
-        piece = lax.reduce_precision(rest, 8, 7)
-        rest = rest - piece
-        part = jnp.dot(mine, piece.astype(bf16), preferred_element_type=f32)
-        pushed = part if pushed is None else pushed + part
-
-    shots, squares = pl.pallas_call(
-        functools.partial(strip_kernel, halo, steps, runs),
+    partial, loss = pl.pallas_call(
+        functools.partial(strip_kernel, halo, steps, runs, scale_of),
         grid=(groups,),
         out_shape=(
-            jax.ShapeDtypeStruct((groups, GROUP * steps, band * wide), bf16),
-            jax.ShapeDtypeStruct((GROUP, LANES), f32),
+            jax.ShapeDtypeStruct((runs * steps, hidden_size), bf16),
+            jax.ShapeDtypeStruct((1, hidden_size), f32),
         ),
-        in_specs=[in_vmem] * (col_size + 3) + [anywhere],
-        out_specs=(
-            pl.BlockSpec((1, GROUP * steps, band * wide), lambda i: (i, 0, 0)),
-            pl.BlockSpec((GROUP, LANES), lambda i: (0, 0)),
-        ),
+        in_specs=[in_vmem] * (col_size + 4) + [anywhere] * 2,
+        out_specs=(in_vmem, in_vmem),
         scratch_shapes=[
             pltpu.VMEM((rows_strip, GROUP, wide), f32),
             pltpu.VMEM((rows_strip, SUB, wide), f32),
             pltpu.VMEM((wide, wide), bf16),
             pltpu.VMEM((wide // LANES, GROUP * rows_strip, LANES), f32),
+            pltpu.VMEM((runs * steps, band * wide), bf16),
+            pltpu.VMEM((hidden_size, -(-band // groups) * groups * wide), bf16),
+            pltpu.VMEM((hidden_size, hidden_size), f32),
+            pltpu.VMEM((GROUP, LANES), f32),
+            pltpu.SemaphoreType.DMA((groups,)),
         ],
-        compiler_params=vmem,
+        compiler_params=vmem(40),
         name="strip_solver",
-    )(*blocks, order, nonlin_wide, counts_wide, field)
-
-    drawn = lax.dot_general(
-        shots.reshape(runs * steps, band * wide), weights, last_dims, preferred_element_type=f32
-    )
-    partial = ((pushed - drawn) * scale_of).astype(bf16)
-    loss = jnp.sum(mine.astype(f32) * (pushed - 2.0 * drawn), axis=0, keepdims=True)
-    loss = loss + jnp.pad(jnp.sum(squares, axis=0, keepdims=True), ((0, 0), (0, hidden_size - LANES)))
+    )(*blocks, order, inverse_wide, counts_wide, mine, weights, field)
 
     cells = row_size * col_size
     share = runs * steps // cells
     pieces = lax.all_to_all(
         partial.reshape(cells, share, hidden_size), ("row", "col"), 0, 0, tiled=True
     )
-    taller = -(-(share + PIECES) // 16) * 16
+    taller = -(-(share + LOSS_PIECES) // 16) * 16
     message_out = pl.pallas_call(
-        functools.partial(share_kernel, scale_of),
+        share_kernel,
         out_shape=jax.ShapeDtypeStruct((cells, taller, hidden_size), bf16),
         in_specs=[in_vmem] * 2,
         out_specs=in_vmem,
-        compiler_params=vmem,
+        compiler_params=vmem(8),
         name="share_sum",
     )(pieces, loss)
     gathered = lax.all_to_all(message_out, ("row", "col"), 0, 0, tiled=True)
@@ -574,7 +625,7 @@
             pltpu.VMEM((rows_all, hidden_size), bf16),
             pltpu.VMEM((run_size, hidden_size), f32),
         ],
-        compiler_params=vmem,
+        compiler_params=vmem(16),
         name="trunk_update",
     )(gathered, other, act, slope, rows_in, w_in, bias_in[None], w_out)
     return (final_field, new_w_in, new_bias[0], new_w_out, mean_loss[0, 0])

time: 170 us -> 136 us (0.80)
  matrix products: 24.1 us -> 3.88 us
  blocking collectives: 17.8 us -> 33.6 us
  Pallas kernels: 76.1 us -> 61.8 us
  waiting for transfers between devices: 12.6 us -> 1.98 us
  starting transfers between devices: 25.3 us -> 18.6 us
  local copies, waits for them, and re-layouts: 7.54 us -> 11.5 us
  other arithmetic: 4.6 us -> 2.59 us
    dot_general x5 -> x0, matrix products: 21.2 us -> none  [the longest x1 10.5 us: per_device(): lax.dot_general(weights, weights, last_dims, preferred_element_type=f32)]
    all_to_all x0 -> x1, blocking collectives: none -> 18.8 us  [per_device(): lax.all_to_all(partial.reshape(cells, share, hidden_size), ('row', 'col')...]
    pallas_call x3 -> x2, Pallas kernels: 36.1 us -> 21.4 us  [the longest x1 21.3 us: per_device(): pl.pallas_call(functools.partial(strip_kernel, halo, steps, runs, scale_o...]
    all_to_all x1 -> x0, waiting for transfers between devices: 10.5 us -> none  [per_device(): lax.all_to_all(partial.reshape(cells, share, hidden_size), ('row', 'col')...]
    all_to_all x1 -> x0, starting transfers between devices: 6.72 us -> none  [per_device(): lax.all_to_all(partial.reshape(cells, share, hidden_size), ('row', 'col')...]
    pallas_call x1, Pallas kernels: 31.8 us -> 35.8 us  [per_device(): pl.pallas_call(functools.partial(tile_kernel, halo, steps, runs), out_sha...]
    all_to_all x1, blocking collectives: 17.8 us -> 14.8 us  [per_device(): gathered = lax.all_to_all(message_out, ('row', 'col'), 0, 0, tiled=True)]
    unnamed x48 -> x36, local copies, waits for them, and re-layouts: 5.13 us -> 7.92 us
  transfers between devices with their start and end apart: 9 -> 8, of which waited for: 3 -> 2; matrix products, arithmetic and copies ran while one was open for 10% -> 5% of each run, Pallas kernels for 27% -> 27%
where the time goes in v1:
time: 136 us; the launch traced here: 135 us
  Pallas kernels  61.8 us (45%)
  blocking collectives  33.6 us (25%)
  starting transfers between devices  18.6 us (14%)
  local copies, waits for them, and re-layouts  11.5 us (8%)
  matrix products  3.88 us (3%)
  other arithmetic  2.59 us (2%)
  waiting for transfers between devices  1.98 us (1%)
    pallas_call x1, Pallas kernels, per_device(): pl.pallas_call(functools.partial(tile_kernel, halo, steps, runs), out_sha...  35.8 us
    pallas_call x1, Pallas kernels, per_device(): pl.pallas_call(functools.partial(strip_kernel, halo, steps, runs, scale_o...  21.3 us
    all_to_all x1, blocking collectives, per_device(): lax.all_to_all(partial.reshape(cells, share, hidden_size), ('row', 'col')...  18.8 us
    all_to_all x1, blocking collectives, per_device(): gathered = lax.all_to_all(message_out, ('row', 'col'), 0, 0, tiled=True)  14.8 us
    ppermute x4, starting transfers between devices, neighbours(): return (lax.ppermute(up, axis, forward), lax.ppermute(down, axis, backward))  12.6 us
    unnamed x36, local copies, waits for them, and re-layouts  7.92 us
    ppermute x3, starting transfers between devices, per_device(): blocks.append(lax.ppermute(messages[hop], 'col', pairs))  5.99 us
  transfers between devices with their start and end apart: 8, of which 2 were waited for; matrix products, arithmetic and copies ran while one was open for 5% of the time, Pallas kernels for 27%

profile of v1, /device:TPU:0, one launch (start us, length us, event | category | flops | bytes accessed | tf_op | source)
XLA Modules:
  0.0 134.9 jit_solution(5574355850565323436)
XLA Ops:
  0.6 0.0 copy-start.16
  0.6 0.0 copy-start.15
  0.7 0.0 copy-start.12
  0.7 0.0 copy-start.10
  0.7 1.8 %fusion.8 = (f32[49,8,128]{2,1,0:T(8,128)}, f32[49,8,128]{2,1,0:T(8,128)S(1)}) fusion(f32[48,64,128]{2,1,0:T(8,128)} %param.13, f32[1,64,128]{2,1,0:T(8,128)} %bitcast.27), kind=kLoop, calls=%fused_computation.20 | loop fusion | flops 100352 | bytes 2007040 | tf_op jit(solution)/shard_map/concatenate | solution.py:496
  2.5 1.3 collective-permute-start.1
  3.7 5.5 %collective-permute-start = (f32[49,8,128]{2,1,0:T(8,128)S(1)}, f32[49,8,128]{2,1,0:T(8,128)S(1)}, u32[]{:S(2)}, u32[]{:S(2)}) collective-permute-start(f32[49,8,128]{2,1,0:T(8,128)S(1)} %get-tuple-element.42), channel_id=1, source_target_pairs={{0,4},{4,8},{8,12},{1,5},{5,9},{9,13},{2,6},{6,10},{10,14},{3,7},{... | collective-permute-start | bytes 602120 | tf_op jit(solution)/shard_map/ppermute | solution.py:24
  9.2 0.0 copy-done.16
  9.3 0.0 copy-done.15
  9.3 0.1 add_convert_fusion
  9.4 0.0 copy-done.12
  9.4 0.0 copy-done.10
  9.4 0.0 copy-start.6
  9.4 2.4 %fusion.6 = (f32[768,512]{1,0:T(8,128)}, bf16[768,512]{1,0:T(8,128)(2,1)S(1)}) fusion(f32[512]{0:T(512)S(1)} %copy-done.12, bf16[768,256]{1,0:T(8,128)(2,1)S(1)} %bitcast.20, bf16[256,512]{1,0:T(8,128)(2,1)S(1)} %copy-done.10), kind=kOutput, calls=%fused_computation.11 | convolution fusion | flops 209190912 | bytes 3016704 | tf_op jit(solution)/shard_map/dot_general | solution.py:564
  11.8 0.0 copy-start
  11.8 0.0 copy-done.6
  11.8 1.4 %convolution_convert_fusion = bf16[768,512]{1,0:T(8,128)(2,1)} fusion(bf16[768,512]{1,0:T(8,128)(2,1)S(1)} %get-tuple-element.44.act_ref, bf16[512,512]{1,0:T(8,128)(2,1)S(1)} %copy-done.6), kind=kOutput, calls=%fused_computation.16 | convolution fusion | flops 403046400 | bytes 2097152 | tf_op jit(solution)/shard_map/dot_general | solution.py:568
  13.3 0.0 copy-done
  13.3 0.0 copy-done.8
  13.3 0.1 fusion
  13.4 0.0 collective-permute-done.1
  13.4 0.1 collective-permute-done
  13.5 2.2 %pack_columns.1 = (f32[5,56,128]{2,1,0:T(8,128)}, f32[5,56,128]{2,1,0:T(8,128)}) custom-call(f32[3072,128]{1,0:T(8,128)S(1)} %bitcast.17, f32[64,128]{1,0:T(8,128)S(1)} %copy-done.8, f32[392,128]{1,0:T(8,128)S(1)} %bitcast.24, f32[392,128]{1,0:T(8,128)S(1)} %bitcast.22), custom_call_target="tpu_custom_call" | custom-call | tf_op jit(solution)/shard_map/pack_columns/pallas_call | solution.py:517
  15.7 0.1 pad_maximum_fusion.1
  15.8 0.0 copy-start.17
  15.8 1.1 constant_dynamic-slice_fusion.1
  17.0 4.6 %collective-permute-start.2 = (f32[5,56,128]{2,1,0:T(8,128)}, f32[5,56,128]{2,1,0:T(8,128)}, u32[]{:S(2)}, u32[]{:S(2)}) collective-permute-start(f32[5,56,128]{2,1,0:T(8,128)} %get-tuple-element.25), channel_id=1, source_target_pairs={{0,1},{1,2},{2,3},{4,5},{5,6},{6,7},{8,9},{9,10},{10,11},{12,13},{... | collective-permute-start | bytes 430088 | tf_op jit(solution)/shard_map/ppermute | solution.py:24
  21.6 1.3 collective-permute-start.3
  22.9 0.0 copy-done.17
  22.9 0.5 broadcast_divide_fusion
  23.4 1.0 constant_dynamic-slice_fusion.refs_7_
  24.4 2.7 %collective-permute-start.4 = (bf16[49,32,128]{2,1,0:T(8,128)(2,1)}, bf16[49,32,128]{2,1,0:T(8,128)(2,1)S(1)}, u32[]{:S(2)}, u32[]{:S(2)}) collective-permute-start(bf16[49,32,128]{2,1,0:T(8,128)(2,1)} %get-tuple-element.29), channel_id=1, source_target_pairs={{0,1},{1,2},{2,3},{3,0},{4,5},{5,6},{6,7},{7,4},{8,9},{9,10},{10,1... | collective-permute-start | bytes 1204232 | tf_op jit(solution)/shard_map/ppermute | solution.py:530
  27.1 2.6 %collective-permute-start.5 = (bf16[49,32,128]{2,1,0:T(8,128)(2,1)}, bf16[49,32,128]{2,1,0:T(8,128)(2,1)S(1)}, u32[]{:S(2)}, u32[]{:S(2)}) collective-permute-start(bf16[49,32,128]{2,1,0:T(8,128)(2,1)} %get-tuple-element.30), channel_id=1, source_target_pairs={{0,2},{1,3},{2,0},{3,1},{4,6},{5,7},{6,4},{7,5},{8,10},{9,11},{10,... | collective-permute-start | bytes 1204232 | tf_op jit(solution)/shard_map/ppermute | solution.py:530
  29.7 0.7 collective-permute-start.6
  30.4 0.0 collective-permute-done.2.left_ref
  30.4 0.0 collective-permute-done.3.right_ref
  30.4 0.7 broadcast_in_dim.9.inverse_ref.refs_5_
  31.1 0.7 broadcast_in_dim.10.counts_ref.refs_6_
  31.9 1.0 copy-done.4
  32.9 0.8 copy-done.9
  33.7 1.3 copy-done.14
  34.9 35.8 %tile_solver.1 = (f32[3072,128]{1,0:T(8,128)}, bf16[512,8192]{1,0:T(8,128)(2,1)}) custom-call(f32[3072,128]{1,0:T(8,128)S(1)} %bitcast.18, f32[64,128]{1,0:T(8,128)S(1)} %copy-done.9, f32[392,128]{1,0:T(8,128)S(1)} %bitcast.25, f32[392,128]{1,0:T(8,128)S(1)} %bitcast.23, f32[5,56,128]{2,1,0:T(8,128)} %collective-permute-done.2.left_ref, ...), custom_call_target="tpu_custom_call" | custom-call | flops 99999997952 | bytes 10000000 | tf_op jit(solution)/shard_map/tile_solver/pallas_call | solution.py:535
  70.8 0.0 collective-permute-done.4.refs_1_
  70.8 0.0 collective-permute-done.5.refs_2_
  70.8 0.0 collective-permute-done.6.refs_3_
  70.8 0.0 copy-done.5
  70.8 0.0 copy-start.1
  70.8 3.4 %copy-done.1 = bf16[512,8192]{1,0:T(8,128)(2,1)S(1)} copy-done((bf16[512,8192]{1,0:T(8,128)(2,1)S(1)}, bf16[512,8192]{1,0:T(8,128)(2,1)}, u32[]{:S(2)}) %copy-start.1) | copy-done | bytes 8388632
  74.2 1.4 %copy-done.2 = f32[3072,128]{1,0:T(8,128)S(1)} copy-done((f32[3072,128]{1,0:T(8,128)S(1)}, f32[3072,128]{1,0:T(8,128)}, u32[]{:S(2)}) %copy-start.2) | copy-done | bytes 1572888
  75.6 21.3 %strip_solver.1 = (bf16[384,512]{1,0:T(8,128)(2,1)S(1)}, f32[1,512]{1,0:T(1,128)S(1)}) custom-call(bf16[49,32,128]{2,1,0:T(8,128)(2,1)S(1)} %get-tuple-element.28.refs_0_, bf16[49,32,128]{2,1,0:T(8,128)(2,1)S(1)} %collective-permute-done.4.refs_1_, bf16[49,32,128]{2,1,0:T(8,128)(2,1)S(1)} %collective-permute-done.5.refs_2_, ...), custom_call_target="tpu_custom_call" | custom-call | tf_op jit(solution)/shard_map/strip_solver/pallas_call | solution.py:572
  96.9 0.0 copy-start.3
  96.9 0.0 copy-start.7
  96.9 0.0 copy-start.11
  96.9 0.0 copy-start.13
  97.0 18.8 %all_to_all.10.pieces_ref = bf16[16,24,512]{2,1,0:T(8,128)(2,1)S(1)} all-to-all(bf16[16,24,512]{2,1,0:T(8,128)(2,1)S(1)} %bitcast.26), channel_id=1, replica_groups=mesh['run'=2,'row'=4,'col'=4] {'row','col'}, dimensions={0} | all-to-all | bytes 786432 | tf_op jit(solution)/shard_map/all_to_all | solution.py:598
  115.7 0.1 share_sum.1
  115.8 14.8 %all_to_all.11.mine_ref = bf16[16,32,512]{2,1,0:T(8,128)(2,1)S(1)} all-to-all(bf16[16,32,512]{2,1,0:T(8,128)(2,1)S(1)} %share_sum.1), channel_id=1, replica_groups=mesh['run'=2,'row'=4,'col'=4] {'row','col'}, dimensions={0} | all-to-all | bytes 1048576 | tf_op jit(solution)/shard_map/all_to_all | solution.py:610
  130.7 0.0 collective-permute-start.7
  130.7 1.9 %collective-permute-done.7.other_ref = bf16[16,32,512]{2,1,0:T(8,128)(2,1)S(1)} collective-permute-done((bf16[16,32,512]{2,1,0:T(8,128)(2,1)S(1)}, bf16[16,32,512]{2,1,0:T(8,128)(2,1)S(1)}, u32[]{:S(2)}, u32[]{:S(2)}) %collective-permute-start.7) | collective-permute-done | bytes 524320 | tf_op jit(solution)/shard_map/ppermute | solution.py:612
  132.6 0.0 copy-done.3
  132.6 0.0 copy-done.7
  132.6 0.0 copy-done.11
  132.6 0.0 copy-done.13
  132.6 2.3 %trunk_update.1 = (f32[256,512]{1,0:T(8,128)}, f32[1,512]{1,0:T(1,128)}, f32[512,512]{1,0:T(8,128)}, f32[1,128]{1,0:T(1,128)}) custom-call(bf16[16,32,512]{2,1,0:T(8,128)(2,1)S(1)} %all_to_all.11.mine_ref, bf16[16,32,512]{2,1,0:T(8,128)(2,1)S(1)} %collective-permute-done.7.other_ref, bf16[768,512]{1,0:T(8,128)(2,1)S(1)} %get-tuple-element.44.act_ref, ...), custom_call_target="tpu_custom_call" | custom-call | tf_op jit(solution)/shard_map/trunk_update/pallas_call | solution.py:614
  (10 shorter events, 0.0 us)
Async XLA Ops:
  0.6 8.6 %copy-start.16 = (bf16[8,256]{1,0:T(8,128)(2,1)S(1)}, bf16[8,256]{1,0:T(8,128)(2,1)}, u32[]{:S(2)}) copy-start(bf16[8,256]{1,0:T(8,128)(2,1)} %param.18) | copy-start | bytes 12292
  0.6 8.6 %copy-start.15 = (bf16[96,256]{1,0:T(8,128)(2,1)S(1)}, bf16[96,256]{1,0:T(8,128)(2,1)}, u32[]{:S(2)}) copy-start(bf16[96,256]{1,0:T(8,128)(2,1)} %param.17) | copy-start | bytes 147460
  0.7 8.7 %copy-start.12 = (f32[512]{0:T(512)S(1)}, f32[512]{0:T(512)}, u32[]{:S(2)}) copy-start(f32[512]{0:T(512)} %param.20) | copy-start | bytes 6148
  0.7 8.7 %copy-start.10 = (bf16[256,512]{1,0:T(8,128)(2,1)S(1)}, bf16[256,512]{1,0:T(8,128)(2,1)}, u32[]{:S(2)}) copy-start(bf16[256,512]{1,0:T(8,128)(2,1)} %w_in_ref.1) | copy-start | bytes 786436
  2.5 10.9 %collective-permute-start.1 = (f32[49,8,128]{2,1,0:T(8,128)}, f32[49,8,128]{2,1,0:T(8,128)S(1)}, u32[]{:S(2)}, u32[]{:S(2)}) collective-permute-start(f32[49,8,128]{2,1,0:T(8,128)} %get-tuple-element.41), channel_id=1, source_target_pairs={{4,0},{8,4},{12,8},{5,1},{9,5},{13,9},{6,2},{10,6},{14,10},{7,3},{... | collective-permute-start | bytes 602120 | tf_op jit(solution)/shard_map/ppermute | solution.py:24
  3.7 9.7 %collective-permute-start = (f32[49,8,128]{2,1,0:T(8,128)S(1)}, f32[49,8,128]{2,1,0:T(8,128)S(1)}, u32[]{:S(2)}, u32[]{:S(2)}) collective-permute-start(f32[49,8,128]{2,1,0:T(8,128)S(1)} %get-tuple-element.42), channel_id=1, source_target_pairs={{0,4},{4,8},{8,12},{1,5},{5,9},{9,13},{2,6},{6,10},{10,14},{3,7},{... | collective-permute-start | bytes 602120 | tf_op jit(solution)/shard_map/ppermute | solution.py:24
  9.4 2.5 %copy-start.6 = (bf16[512,512]{1,0:T(8,128)(2,1)S(1)}, bf16[512,512]{1,0:T(8,128)(2,1)}, u32[]{:S(2)}) copy-start(bf16[512,512]{1,0:T(8,128)(2,1)} %w_out_ref.1) | copy-start | bytes 1572868
  11.8 1.5 %copy-start = (f32[48,64,128]{2,1,0:T(8,128)S(1)}, f32[48,64,128]{2,1,0:T(8,128)}, u32[]{:S(2)}) copy-start(f32[48,64,128]{2,1,0:T(8,128)} %param.13) | copy-start | bytes 4718596
  11.8 1.5 %copy-start.8 = (f32[64,128]{1,0:T(8,128)S(1)}, f32[64,128]{1,0:T(8,128)}, u32[]{:S(2)}) copy-start(f32[64,128]{1,0:T(8,128)} %cond_ref.3) | copy-start | bytes 98308
  15.8 7.1 %copy-start.17 = (f32[48]{0:T(128)S(1)}, f32[48]{0:T(128)}, u32[]{:S(2)}) copy-start(f32[48]{0:T(128)} %param.15) | copy-start | bytes 580
  17.0 13.4 %collective-permute-start.2 = (f32[5,56,128]{2,1,0:T(8,128)}, f32[5,56,128]{2,1,0:T(8,128)}, u32[]{:S(2)}, u32[]{:S(2)}) collective-permute-start(f32[5,56,128]{2,1,0:T(8,128)} %get-tuple-element.25), channel_id=1, source_target_pairs={{0,1},{1,2},{2,3},{4,5},{5,6},{6,7},{8,9},{9,10},{10,11},{12,13},{... | collective-permute-start | bytes 430088 | tf_op jit(solution)/shard_map/ppermute | solution.py:24
  21.6 8.8 %collective-permute-start.3 = (f32[5,56,128]{2,1,0:T(8,128)}, f32[5,56,128]{2,1,0:T(8,128)}, u32[]{:S(2)}, u32[]{:S(2)}) collective-permute-start(f32[5,56,128]{2,1,0:T(8,128)} %get-tuple-element.26), channel_id=1, source_target_pairs={{1,0},{2,1},{3,2},{5,4},{6,5},{7,6},{9,8},{10,9},{11,10},{13,12},{... | collective-permute-start | bytes 430088 | tf_op jit(solution)/shard_map/ppermute | solution.py:24
  24.4 46.4 %collective-permute-start.4 = (bf16[49,32,128]{2,1,0:T(8,128)(2,1)}, bf16[49,32,128]{2,1,0:T(8,128)(2,1)S(1)}, u32[]{:S(2)}, u32[]{:S(2)}) collective-permute-start(bf16[49,32,128]{2,1,0:T(8,128)(2,1)} %get-tuple-element.29), channel_id=1, source_target_pairs={{0,1},{1,2},{2,3},{3,0},{4,5},{5,6},{6,7},{7,4},{8,9},{9,10},{10,1... | collective-permute-start | bytes 1204232 | tf_op jit(solution)/shard_map/ppermute | solution.py:530
  27.1 43.7 %collective-permute-start.5 = (bf16[49,32,128]{2,1,0:T(8,128)(2,1)}, bf16[49,32,128]{2,1,0:T(8,128)(2,1)S(1)}, u32[]{:S(2)}, u32[]{:S(2)}) collective-permute-start(bf16[49,32,128]{2,1,0:T(8,128)(2,1)} %get-tuple-element.30), channel_id=1, source_target_pairs={{0,2},{1,3},{2,0},{3,1},{4,6},{5,7},{6,4},{7,5},{8,10},{9,11},{10,... | collective-permute-start | bytes 1204232 | tf_op jit(solution)/shard_map/ppermute | solution.py:530
  29.7 41.1 %collective-permute-start.6 = (bf16[49,32,128]{2,1,0:T(8,128)(2,1)}, bf16[49,32,128]{2,1,0:T(8,128)(2,1)S(1)}, u32[]{:S(2)}, u32[]{:S(2)}) collective-permute-start(bf16[49,32,128]{2,1,0:T(8,128)(2,1)} %get-tuple-element.31), channel_id=1, source_target_pairs={{0,3},{1,0},{2,1},{3,2},{4,7},{5,4},{6,5},{7,6},{8,11},{9,8},{10,9... | collective-permute-start | bytes 1204232 | tf_op jit(solution)/shard_map/ppermute | solution.py:530
  31.9 1.0 copy-start.4
  32.9 0.8 copy-start.9
  33.7 1.3 copy-start.14
  34.9 35.9 %copy-start.5 = (bf16[512,512]{1,0:T(8,128)(2,1)S(1)}, bf16[512,512]{1,0:T(8,128)(2,1)}, u32[]{:S(2)}) copy-start(bf16[512,512]{1,0:T(8,128)(2,1)} %constant.70.clone.order_ref.refs_4_) | copy-start | bytes 1572868
  70.8 3.4 %copy-start.1 = (bf16[512,8192]{1,0:T(8,128)(2,1)S(1)}, bf16[512,8192]{1,0:T(8,128)(2,1)}, u32[]{:S(2)}) copy-start(bf16[512,8192]{1,0:T(8,128)(2,1)} %get-tuple-element.33.refs_8_) | copy-start | bytes 25165828
  74.2 1.4 %copy-start.2 = (f32[3072,128]{1,0:T(8,128)S(1)}, f32[3072,128]{1,0:T(8,128)}, u32[]{:S(2)}) copy-start(f32[3072,128]{1,0:T(8,128)} %get-tuple-element.27.refs_9_) | copy-start | bytes 4718596
  96.9 35.7 %copy-start.3 = (f32[768,512]{1,0:T(8,128)S(1)}, f32[768,512]{1,0:T(8,128)}, u32[]{:S(2)}) copy-start(f32[768,512]{1,0:T(8,128)} %get-tuple-element.36.slope_ref) | copy-start | bytes 4718596
  96.9 35.6 %copy-start.7 = (bf16[512,512]{1,0:T(8,128)(2,1)S(1)}, bf16[512,512]{1,0:T(8,128)(2,1)}, u32[]{:S(2)}) copy-start(bf16[512,512]{1,0:T(8,128)(2,1)} %w_out_ref.1) | copy-start | bytes 1572868
  96.9 35.6 %copy-start.11 = (bf16[256,512]{1,0:T(8,128)(2,1)S(1)}, bf16[256,512]{1,0:T(8,128)(2,1)}, u32[]{:S(2)}) copy-start(bf16[256,512]{1,0:T(8,128)(2,1)} %w_in_ref.1) | copy-start | bytes 786436
  96.9 35.6 %copy-start.13 = (f32[512]{0:T(512)S(1)}, f32[512]{0:T(512)}, u32[]{:S(2)}) copy-start(f32[512]{0:T(512)} %param.20) | copy-start | bytes 6148
  130.7 1.9 %collective-permute-start.7 = (bf16[16,32,512]{2,1,0:T(8,128)(2,1)S(1)}, bf16[16,32,512]{2,1,0:T(8,128)(2,1)S(1)}, u32[]{:S(2)}, u32[]{:S(2)}) collective-permute-start(bf16[16,32,512]{2,1,0:T(8,128)(2,1)S(1)} %all_to_all.11.mine_ref), channel_id=1, source_target_pairs={{0,16},{16,0},{1,17},{17,1},{2,18},{18,2},{3,19},{19,3},{4,20},{20... | collective-permute-start | bytes 1572872 | tf_op jit(solution)/shard_map/ppermute | solution.py:612

commit v2 on v1

--- a/solution.py
+++ b/solution.py
@@ -11,6 +11,7 @@
 time_step = 0.12
 learn_rate = 0.5
 LANES = 128
+FRONT_PARTS = 2
 SUB = 8
 GROUP = 16
 f32 = jnp.float32
@@ -28,6 +29,14 @@
     return cond * pltpu.reciprocal(inverse + u * u, approx=True)
 
 
+def spread(ref, first, count):
+    at = lax.broadcasted_iota(jnp.int32, (count, LANES), 0)
+    value = jnp.full((count, LANES), ref[first])
+    for i in range(1, count):
+        value = jnp.where(at == i, ref[first + i], value)
+    return value
+
+
 def apart(wide):
     parts = wide // LANES
     source = np.arange(wide)[:, None]
@@ -35,10 +44,10 @@
     return jnp.asarray(source == parts * (place % LANES) + place // LANES, bf16)
 
 
-def reorder(index, size, d_ref, order_ref, out_ref, wide_ref):
+def reorder(source, target, size, d_ref, order_ref, out_ref, wide_ref):
     _, band, wide = d_ref.shape
-    here = pl.ds(pl.multiple_of(index * size, size), size)
-    x = d_ref[here]
+    here = pl.ds(pl.multiple_of(target * size, size), size)
+    x = d_ref[pl.ds(pl.multiple_of(source * size, size), size)]
     if band % 16:
         x = x.astype(f32).reshape(size * band, wide).astype(bf16)
     else:
@@ -68,6 +77,7 @@
 
 
 ROW_SEGS = 8
+COND_ROWS = 16
 COL_SEGS = 16
 
 
@@ -150,56 +160,69 @@
     return pieces
 
 
-def tile_kernel(
-    halo, steps, runs, x_ref, cond_ref, top_ref, bottom_ref, left_ref, right_ref, inverse_ref,
-    counts_ref, main_ref, edge_ref, order_ref, decoder_hbm, out_ref, weights_hbm, u_ref, c_ref,
-    rate_ref, body_ref, ends_ref, back_ref, decoder_ref, weights_ref, part_ref, sems,
-):
-    fetch = pltpu.make_async_copy(decoder_hbm, decoder_ref, sems.at[0])
-    fetch.start()
+def tile_kernel(part, halo, steps, runs, *refs):
+    x_ref, cond_ref, top_ref, bottom_ref, left_ref, right_ref, nonlin_ref, counts_ref = refs[:8]
+    main_ref, edge_ref = refs[8:10]
+    out_ref, u_ref, c_ref, rate_ref, body_ref, ends_ref, back_ref, pad_ref = refs[-8:]
     rows_dev, cols_dev = cond_ref.shape
-    source = row_source(halo, rows_dev, runs, (x_ref, cond_ref, top_ref, bottom_ref))
     deep = (rows_dev + 2 * halo) // ROW_SEGS
     across = (cols_dev + 2 * halo) // COL_SEGS
-    tall = runs + GROUP
+    packs = left_ref.shape[0]
+    first_run = part * GROUP
     row_at, row_count = lax.axis_index("row"), lax.axis_size("row")
     col_at, col_count = lax.axis_index("col"), lax.axis_size("col")
 
-    for b in range(deep):
-        for seg in range(ROW_SEGS):
-            for i, piece in enumerate(pieces_of(source(seg * deep + b, GROUP))):
-                body_ref[i, b * tall : (b + 1) * tall, seg * cols_dev : (seg + 1) * cols_dev] = piece
-        for side, ref in enumerate((left_ref, right_ref)):
-            value = jnp.concatenate([ref[b // 2], ref[b // 2, runs:]], axis=0)
-            for i, piece in enumerate(pieces_of(value)):
-                first = b // 2 * tall
-                ends_ref[i, b % 2, first : first + tall, side * LANES : (side + 1) * LANES] = piece
+    def source(row):
+        if row < halo:
+            return top_ref[pl.ds(first_run * halo + row, GROUP, stride=halo), :]
+        row -= halo
+        if row < rows_dev:
+            return x_ref[pl.ds(row, GROUP, stride=rows_dev), :]
+        return bottom_ref[pl.ds(first_run * halo + row - rows_dev, GROUP, stride=halo), :]
+
+    pad_ref[...] = jnp.zeros_like(pad_ref)
+    pad_ref[:halo] = top_ref[runs * halo : (runs + 1) * halo]
+    pad_ref[halo : halo + rows_dev] = cond_ref[...]
+    pad_ref[halo + rows_dev : 2 * halo + rows_dev] = bottom_ref[runs * halo : (runs + 1) * halo]
+    for seg in range(ROW_SEGS):
+        lanes = slice(seg * cols_dev, (seg + 1) * cols_dev)
+        for b in range(deep):
+            for i, piece in enumerate(pieces_of(source(seg * deep + b))):
+                body_ref[i, b * GROUP : (b + 1) * GROUP, lanes] = piece
+        for i, piece in enumerate(pieces_of(pad_ref[seg * deep : seg * deep + COND_ROWS])):
+            body_ref[i, deep * GROUP : deep * GROUP + COND_ROWS, lanes] = piece
+    for side, ref in enumerate((left_ref, right_ref)):
+        lanes = slice(side * LANES, (side + 1) * LANES)
+        for block in range(packs):
+            for i, piece in enumerate(pieces_of(ref[block, first_run : first_run + GROUP])):
+                ends_ref[i, block * GROUP : (block + 1) * GROUP, lanes] = piece
+        conds = [ref[block, runs : runs + 1] for block in range(packs)]
+        conds.append(jnp.zeros((COND_ROWS - packs, LANES), f32))
+        for i, piece in enumerate(pieces_of(jnp.concatenate(conds, axis=0))):
+            ends_ref[i, packs * GROUP : packs * GROUP + COND_ROWS, lanes] = piece
 
     lane = lax.broadcasted_iota(jnp.int32, (SUB, LANES), 1)
     chunk = 3 if across % 3 == 0 else 1
     for start in range(0, across, chunk):
         lanes = slice(start * LANES, (start + chunk) * LANES)
         total = None
+        extra = [None, None]
         for i in range(PIECES):
-            part = jnp.dot(body_ref[i], main_ref[:, lanes], preferred_element_type=f32)
-            total = part if total is None else total + part
-        extra = []
-        for parity in range(2):
-            more = None
-            for i in range(PIECES):
-                part = jnp.dot(
-                    ends_ref[i, parity], edge_ref[parity, :, lanes], preferred_element_type=f32
-                )
-                more = part if more is None else more + part
-            extra.append(more)
+            more = jnp.dot(body_ref[i], main_ref[:, lanes], preferred_element_type=f32)
+            total = more if total is None else total + more
+            for parity in range(2):
+                more = jnp.dot(ends_ref[i], edge_ref[parity, :, lanes], preferred_element_type=f32)
+                extra[parity] = more if extra[parity] is None else extra[parity] + more
         for b in range(deep):
-            first = b // 2 * tall
-            value = total[b * tall : (b + 1) * tall] + extra[b % 2][first : first + tall]
+            first = b // 2 * GROUP
+            value = total[b * GROUP : (b + 1) * GROUP] + extra[b % 2][first : first + GROUP]
+            at = packs * GROUP + b // 2
+            cond = total[deep * GROUP + b : deep * GROUP + b + 1] + extra[b % 2][at : at + 1]
             for inner in range(chunk):
                 q = start + inner
-                here = value[:, inner * LANES : (inner + 1) * LANES]
-                u_ref[0, b, q] = here[:runs]
-                c_ref[b + 1, q] = here[runs : runs + SUB]
+                here = slice(inner * LANES, (inner + 1) * LANES)
+                u_ref[0, b, q] = value[:, here]
+                c_ref[b + 1, q] = jnp.broadcast_to(cond[:, here], (SUB, LANES))
     for b in range(deep):
         for q in range(across):
             row = lane // COL_SEGS * deep + b
@@ -215,15 +238,10 @@
         c_ref[0, q] = pltpu.roll(c_ref[deep, q], COL_SEGS, 1)
         c_ref[deep + 1, q] = pltpu.roll(c_ref[1, q], LANES - COL_SEGS, 1)
 
-    size = part_ref.shape[1] // decoder_ref.shape[1]
-    chunks = decoder_ref.shape[0] // size
-    each = -(-chunks // (runs // SUB))
-    fetch.wait()
-
     def group(index, _):
         where = pl.ds(pl.multiple_of(index * SUB, SUB), SUB)
-        inverse = inverse_ref[where, :]
-        counts = counts_ref[where, :]
+        inverse = 1.0 / spread(nonlin_ref, first_run + index * SUB, SUB)
+        counts = spread(counts_ref, first_run + index * SUB, SUB)
 
         def step(number, old, new):
             active = jnp.where(number < counts, inverse, 0.0)
@@ -254,48 +272,48 @@
                     u_ref[new, b, q, where, :] = u[q] + (rate_ref[b, q] * active) * flux
                 here, below = then, above
 
-        done = 0
-        for number in range(steps):
-            step(number, number % 2, 1 - number % 2)
-            while done < each * (number + 1) // steps:
-                chunk = jnp.minimum(index * each + done, chunks - 1)
-                reorder(chunk, size, decoder_ref, order_ref, weights_ref, part_ref)
-                done += 1
+        def two(i, _):
+            step(2 * i, 0, 1)
+            step(2 * i + 1, 1, 0)
+            return 0
+
+        lax.fori_loop(0, steps // 2, two, 0)
         return 0
 
-    lax.fori_loop(0, runs // SUB, group, 0)
-    store = pltpu.make_async_copy(weights_ref, weights_hbm, sems.at[1])
-    store.start()
+    lax.fori_loop(0, GROUP // SUB, group, 0)
 
     for b in range(deep):
         for q in range(across):
-            for i, piece in enumerate(pieces_of(u_ref[steps % 2, b, q])):
-                back_ref[i, b * runs : (b + 1) * runs, q * LANES : (q + 1) * LANES] = piece
+            for i, piece in enumerate(pieces_of(u_ref[0, b, q])):
+                back_ref[i, b * GROUP : (b + 1) * GROUP, q * LANES : (q + 1) * LANES] = piece
     chunk = 2 if ROW_SEGS % 2 == 0 else 1
     for start in range(0, ROW_SEGS, chunk):
         places = slice(start * cols_dev, (start + chunk) * cols_dev)
         total = None
         for i in range(PIECES):
-            part = lax.dot_general(
+            more = lax.dot_general(
                 back_ref[i], main_ref[places, :], (((1,), (1,)), ((), ())), preferred_element_type=f32
             )
-            total = part if total is None else total + part
+            total = more if total is None else total + more
         for b in range(deep):
             for inner in range(chunk):
                 row = (start + inner) * deep + b - halo
                 if 0 <= row < rows_dev:
-                    out_ref[pl.ds(row, runs, stride=rows_dev), :] = total[
-                        b * runs : (b + 1) * runs, inner * cols_dev : (inner + 1) * cols_dev
+                    out_ref[pl.ds(row, GROUP, stride=rows_dev), :] = total[
+                        b * GROUP : (b + 1) * GROUP, inner * cols_dev : (inner + 1) * cols_dev
                     ]
-    store.wait()
+
+
+def decoder_kernel(d_ref, order_ref, out_ref, wide_ref):
+    reorder(0, 0, d_ref.shape[0], d_ref, order_ref, out_ref, wide_ref)
 
 
 def strip_kernel(halo, steps, runs, scale_of, *refs):
     count = lax.axis_size("col")
     blocks = refs[:count]
-    order_ref, inverse_ref, counts_ref, hidden_ref, weights_hbm = refs[count : count + 5]
-    out_ref, loss_ref, u_ref, c_ref, turned_ref, wide_ref = refs[count + 6 : count + 12]
-    shot_ref, weights_ref, gram_ref, square_ref, sems = refs[count + 12 :]
+    order_ref, nonlin_ref, counts_ref, hidden_ref, weights_hbm = refs[count : count + 5]
+    out_ref, loss_ref, u_ref, c_ref, turned_ref, wide_ref = refs[count + 5 : count + 11]
+    shot_ref, weights_ref, gram_ref, square_ref, sems = refs[count + 11 :]
     cols_dev = blocks[0].shape[2]
     wide = count * cols_dev
     parts = wide // LANES
@@ -357,8 +375,8 @@
         for part in range(parts):
             lanes = pl.ds(part * LANES, LANES)
             u_ref[row, :, lanes] = wide_ref[part, pl.ds(row, GROUP, stride=rows), :]
-    inverse = inverse_ref[where, :]
-    counts = counts_ref[where, :]
+    inverse = 1.0 / spread(nonlin_ref, index * GROUP, GROUP)
+    counts = spread(counts_ref, index * GROUP, GROUP)
     first_row = pl.multiple_of(index * GROUP * steps, GROUP)
 
     def get(row):
@@ -411,13 +429,15 @@
 
     @pl.when(index == pl.num_programs(0) - 1)
     def _():
+        size = runs * steps
+        hidden = hidden_ref[pl.ds(pl.multiple_of(lax.axis_index("run") * size, size), size), :]
         pushed = None
         for piece in pieces_of(gram_ref[...]):
-            part = jnp.dot(hidden_ref[...], piece, preferred_element_type=f32)
+            part = jnp.dot(hidden, piece, preferred_element_type=f32)
             pushed = part if pushed is None else pushed + part
         drawn = product(shot_ref, weights_ref)
         out_ref[...] = ((pushed - drawn) * scale_of).astype(bf16)
-        loss = jnp.sum(hidden_ref[...].astype(f32) * (pushed - 2.0 * drawn), axis=0, keepdims=True)
+        loss = jnp.sum(hidden.astype(f32) * (pushed - 2.0 * drawn), axis=0, keepdims=True)
         loss_ref[...] = loss
         loss_ref[:, :LANES] += jnp.sum(square_ref[...], axis=0, keepdims=True)
 
@@ -491,7 +511,8 @@
         return pltpu.CompilerParams(vmem_limit_bytes=mib * 1024 * 1024)
 
     in_vmem = pl.BlockSpec(memory_space=pltpu.VMEM)
-    anywhere = pl.BlockSpec(memory_space=pl.ANY)
+    in_hbm = pl.BlockSpec(memory_space=pltpu.HBM)
+    in_smem = pl.BlockSpec(memory_space=pltpu.SMEM)
 
     tile = jnp.concatenate([init_field, conduct[None]], axis=0)
     top, bottom = neighbours(tile[:, rows_dev - halo :], tile[:, :halo], "row")
@@ -506,7 +527,6 @@
 
     deep = (rows_dev + 2 * halo) // ROW_SEGS
     across = (cols_dev + 2 * halo) // COL_SEGS
-    tall = runs + GROUP
     tile_args = (
         init_field.reshape(runs * rows_dev, cols_dev),
         conduct,
@@ -519,44 +539,62 @@
         out_shape=(pack_shape, pack_shape),
         in_specs=[in_vmem] * 4,
         out_specs=(in_vmem, in_vmem),
-        compiler_params=vmem(8),
+        compiler_params=vmem(6),
         name="pack_columns",
     )(*tile_args)
-    (low, high), messages = lax.optimization_barrier(((low, high), messages))
+    order = apart(wide)
+    (low, high, order), messages = lax.optimization_barrier(((low, high, order), messages))
     left, right = neighbours(high, low, "col")
     blocks = messages[:1]
     for hop in range(1, col_size):
         pairs = [(i, (i + hop) % col_size) for i in range(col_size)]
         blocks.append(lax.ppermute(messages[hop], "col", pairs))
 
-    inverse_wide = jnp.broadcast_to(1.0 / nonlin[:, None], (runs, LANES))
-    counts_wide = jnp.broadcast_to(counts[:, None], (runs, LANES))
-    order = apart(wide)
-    field, weights = pl.pallas_call(
-        functools.partial(tile_kernel, halo, steps, runs),
-        out_shape=(
-            jax.ShapeDtypeStruct((runs * rows_dev, cols_dev), f32),
-            jax.ShapeDtypeStruct((hidden_size, band * wide), bf16),
-        ),
-        in_specs=[in_vmem] * 11 + [anywhere],
-        out_specs=(in_vmem, anywhere),
-        scratch_shapes=[
-            pltpu.VMEM((2, deep, across, runs, LANES), f32),
-            pltpu.VMEM((deep + 2, across, SUB, LANES), f32),
-            pltpu.VMEM((deep, across, SUB, LANES), f32),
-            pltpu.VMEM((PIECES, deep * tall, ROW_SEGS * cols_dev), bf16),
-            pltpu.VMEM((PIECES, 2, -(-deep // 2) * tall, 2 * LANES), bf16),
-            pltpu.VMEM((PIECES, deep * runs, across * LANES), bf16),
-            pltpu.VMEM(decoder.shape, bf16),
-            pltpu.VMEM((hidden_size, band * wide), bf16),
-            pltpu.VMEM((wide // LANES, 32 * band, LANES), f32),
-            pltpu.SemaphoreType.DMA((2,)),
-        ],
-        compiler_params=vmem(48),
-        cost_estimate=pl.CostEstimate(flops=10**11, bytes_accessed=10**7, transcendentals=0),
-        name="tile_solver",
-    )(*tile_args, left, right, inverse_wide, counts_wide, *tile_order(halo, cols_dev), order, decoder)
-    final_field = field.reshape(init_field.shape)
+    size = 64
+    weights = pl.pallas_call(
+        decoder_kernel,
+        grid=(hidden_size // size,),
+        out_shape=jax.ShapeDtypeStruct((hidden_size, band * wide), bf16),
+        in_specs=[pl.BlockSpec((size, band, wide), lambda i: (i, 0, 0)), in_vmem],
+        out_specs=pl.BlockSpec((size, band * wide), lambda i: (i, 0)),
+        scratch_shapes=[pltpu.VMEM((wide // LANES, size * band, LANES), f32)],
+        compiler_params=vmem(12),
+        cost_estimate=pl.CostEstimate(flops=10**10, bytes_accessed=10**7, transcendentals=0),
+        name="decoder_order",
+    )(decoder, order)
+
+    main, edge = tile_order(halo, cols_dev)
+
+    def solve(part, left, right, done):
+        block = pl.BlockSpec((GROUP * rows_dev, cols_dev), lambda i: (part, 0))
+        packs = left.shape[0]
+        return pl.pallas_call(
+            functools.partial(tile_kernel, part, halo, steps, runs),
+            grid=(1,),
+            out_shape=jax.ShapeDtypeStruct((runs * rows_dev, cols_dev), f32),
+            in_specs=[block] + [in_vmem] * 5 + [in_smem] * 2 + [in_vmem] * 2 + [in_hbm] * len(done),
+            out_specs=block,
+            scratch_shapes=[
+                pltpu.VMEM((2, deep, across, GROUP, LANES), f32),
+                pltpu.VMEM((deep + 2, across, SUB, LANES), f32),
+                pltpu.VMEM((deep, across, SUB, LANES), f32),
+                pltpu.VMEM((PIECES, deep * GROUP + COND_ROWS, ROW_SEGS * cols_dev), bf16),
+                pltpu.VMEM((PIECES, packs * GROUP + COND_ROWS, 2 * LANES), bf16),
+                pltpu.VMEM((PIECES, deep * GROUP, across * LANES), bf16),
+                pltpu.VMEM((rows_dev + 2 * halo + COND_ROWS, cols_dev), f32),
+            ],
+            input_output_aliases={10: 0} if done else {},
+            compiler_params=vmem(14),
+            cost_estimate=pl.CostEstimate(
+                flops=10**10 if done else 10**11, bytes_accessed=10**7, transcendentals=0
+            ),
+            name="tile_solver",
+        )(*tile_args, left, right, nonlin, counts, main, edge, *done)
+
+    early = FRONT_PARTS
+    field = ()
+    for part in range(early):
+        field = (solve(part, left, right, field),)
 
     desc = descriptors.astype(f32).reshape(run_size * groups, 1, GROUP, -1)
     codes = time_code.astype(f32)[None, :, None, :]
@@ -567,8 +605,7 @@
     act = act.astype(bf16)
     hidden = jnp.dot(act, w_out, preferred_element_type=f32).astype(bf16)
     hidden, slope = lax.optimization_barrier((hidden, slope))
-    mine = lax.dynamic_slice_in_dim(hidden, lax.axis_index("run") * runs * steps, runs * steps, 0)
-
+    hidden, *field = lax.optimization_barrier((hidden, *field))
     partial, loss = pl.pallas_call(
         functools.partial(strip_kernel, halo, steps, runs, scale_of),
         grid=(groups,),
@@ -576,7 +613,7 @@
             jax.ShapeDtypeStruct((runs * steps, hidden_size), bf16),
             jax.ShapeDtypeStruct((1, hidden_size), f32),
         ),
-        in_specs=[in_vmem] * (col_size + 4) + [anywhere] * 2,
+        in_specs=[in_vmem] * (col_size + 1) + [in_smem] * 2 + [in_vmem, in_hbm],
         out_specs=(in_vmem, in_vmem),
         scratch_shapes=[
             pltpu.VMEM((rows_strip, GROUP, wide), f32),
@@ -589,25 +626,34 @@
             pltpu.VMEM((GROUP, LANES), f32),
             pltpu.SemaphoreType.DMA((groups,)),
         ],
-        compiler_params=vmem(40),
+        compiler_params=vmem(30),
         name="strip_solver",
-    )(*blocks, order, inverse_wide, counts_wide, mine, weights, field)
+    )(*blocks, order, nonlin, counts, hidden, weights)
 
     cells = row_size * col_size
     share = runs * steps // cells
+    partial, left, right = lax.optimization_barrier((partial, left, right))
+    for part in range(early, groups - 1):
+        field = (solve(part, left, right, field),)
     pieces = lax.all_to_all(
         partial.reshape(cells, share, hidden_size), ("row", "col"), 0, 0, tiled=True
     )
     taller = -(-(share + LOSS_PIECES) // 16) * 16
+    pieces, *field = lax.optimization_barrier((pieces, *field))
     message_out = pl.pallas_call(
         share_kernel,
         out_shape=jax.ShapeDtypeStruct((cells, taller, hidden_size), bf16),
         in_specs=[in_vmem] * 2,
         out_specs=in_vmem,
-        compiler_params=vmem(8),
+        compiler_params=vmem(4),
         name="share_sum",
     )(pieces, loss)
+    message_out, left, right = lax.optimization_barrier((message_out, left, right))
+    if early < groups:
+        field = (solve(groups - 1, left, right, field),)
+    final_field = field[0].reshape(init_field.shape)
     gathered = lax.all_to_all(message_out, ("row", "col"), 0, 0, tiled=True)
+    gathered, final_field = lax.optimization_barrier((gathered, final_field))
     swap = [(i, (i + 1) % run_size) for i in range(run_size)]
     other = lax.ppermute(gathered, "run", swap)
     cells_total = rows_dev * row_size * wide
@@ -625,7 +671,7 @@
             pltpu.VMEM((rows_all, hidden_size), bf16),
             pltpu.VMEM((run_size, hidden_size), f32),
         ],
-        compiler_params=vmem(16),
+        compiler_params=vmem(12),
         name="trunk_update",
     )(gathered, other, act, slope, rows_in, w_in, bias_in[None], w_out)
     return (final_field, new_w_in, new_bias[0], new_w_out, mean_loss[0, 0])

time: 136 us -> 129 us (0.949)
  blocking collectives: 33.6 us -> 19.4 us
  starting transfers between devices: 18.6 us -> 22.5 us
  Pallas kernels: 61.8 us -> 65.4 us
    all_to_all x1 -> x0, blocking collectives: 14.8 us -> none  [per_device(): gathered = lax.all_to_all(message_out, ('row', 'col'), 0, 0, tiled=True)]
    unnamed x36 -> x48, local copies, waits for them, and re-layouts: 7.92 us -> 12.6 us
    all_to_all x0 -> x1, starting transfers between devices: none -> 3.83 us  [per_device(): gathered = lax.all_to_all(message_out, ('row', 'col'), 0, 0, tiled=True)]
    pallas_call x1 -> x4, Pallas kernels: 35.8 us -> 38.6 us  [the longest x3 27.4 us: solve(): pl.pallas_call(functools.partial(tile_kernel, part, halo, steps, runs), g...]
    broadcast_in_dim x2 -> x0, local copies, waits for them, and re-layouts: 1.45 us -> none  [the longest x1 0.73 us: per_device(): counts_wide = jnp.broadcast_to(counts[:, None], (runs, LANES))]
  transfers between devices with their start and end apart: 8 -> 9, of which waited for: 2 -> 1; matrix products, arithmetic and copies ran while one was open for 5% -> 3% of each run, Pallas kernels for 27% -> 30%
where the time goes in v2:
time: 129 us; the launch traced here: 128 us
  Pallas kernels  65.4 us (51%)
  starting transfers between devices  22.5 us (17%)
  blocking collectives  19.4 us (15%)
  local copies, waits for them, and re-layouts  12.8 us (10%)
  matrix products  3.89 us (3%)
  waiting for transfers between devices  1.93 us (1%)
  other arithmetic  1.39 us (1%)
    pallas_call x3, Pallas kernels, solve(): pl.pallas_call(functools.partial(tile_kernel, part, halo, steps, runs), g...  27.4 us
    pallas_call x1, Pallas kernels, per_device(): pl.pallas_call(functools.partial(strip_kernel, halo, steps, runs, scale_o...  22.1 us
    all_to_all x1, blocking collectives, per_device(): lax.all_to_all(partial.reshape(cells, share, hidden_size), ('row', 'col')...  19.4 us
    unnamed x48, local copies, waits for them, and re-layouts  12.6 us
    ppermute x4, starting transfers between devices, neighbours(): return (lax.ppermute(up, axis, forward), lax.ppermute(down, axis, backward))  12.1 us
    pallas_call x1, Pallas kernels, per_device(): pl.pallas_call(decoder_kernel, grid=(hidden_size // size,), out_shape=jax...  11.2 us
    ppermute x3, starting transfers between devices, per_device(): blocks.append(lax.ppermute(messages[hop], 'col', pairs))  6.62 us
    all_to_all x1, starting transfers between devices, per_device(): gathered = lax.all_to_all(message_out, ('row', 'col'), 0, 0, tiled=True)  3.83 us
  transfers between devices with their start and end apart: 9, of which 1 were waited for; matrix products, arithmetic and copies ran while one was open for 3% of the time, Pallas kernels for 30%

profile of v2, /device:TPU:0, one launch (start us, length us, event | category | flops | bytes accessed | tf_op | source)
XLA Modules:
  0.0 128.3 jit_solution(13997569456659390355)
XLA Ops:
  0.6 0.0 copy-start.23
  0.6 0.0 copy-start.22
  0.7 0.0 copy-start.10
  0.7 0.0 copy-start.8
  0.7 1.1 fusion.8
  1.8 1.3 %collective-permute-start.1 = (f32[49,8,128]{2,1,0:T(8,128)S(1)}, f32[49,8,128]{2,1,0:T(8,128)S(1)}, u32[]{:S(2)}, u32[]{:S(2)}) collective-permute-start(f32[49,8,128]{2,1,0:T(8,128)S(1)} %get-tuple-element.63), channel_id=1, source_target_pairs={{4,0},{8,4},{12,8},{5,1},{9,5},{13,9},{6,2},{10,6},{14,10},{7,3},{... | collective-permute-start | bytes 602120 | tf_op jit(solution)/shard_map/ppermute | solution.py:25
  3.1 5.5 %collective-permute-start = (f32[49,8,128]{2,1,0:T(8,128)S(1)}, f32[49,8,128]{2,1,0:T(8,128)S(1)}, u32[]{:S(2)}, u32[]{:S(2)}) collective-permute-start(f32[49,8,128]{2,1,0:T(8,128)S(1)} %get-tuple-element.64), channel_id=1, source_target_pairs={{0,4},{4,8},{8,12},{1,5},{5,9},{9,13},{2,6},{6,10},{10,14},{3,7},{... | collective-permute-start | bytes 602120 | tf_op jit(solution)/shard_map/ppermute | solution.py:25
  8.6 0.0 copy-done.23
  8.6 0.0 copy-done.22
  8.6 0.1 add_convert_fusion
  8.7 0.0 copy-done.10
  8.7 0.0 copy-done.8
  8.7 0.0 copy-start.6
  8.7 2.4 %fusion.6 = (f32[768,512]{1,0:T(8,128)}, bf16[768,512]{1,0:T(8,128)(2,1)S(1)}) fusion(f32[512]{0:T(512)S(1)} %copy-done.10, bf16[768,256]{1,0:T(8,128)(2,1)S(1)} %bitcast.21, bf16[256,512]{1,0:T(8,128)(2,1)S(1)} %copy-done.8), kind=kOutput, calls=%fused_computation.11 | convolution fusion | flops 209190912 | bytes 3016704 | tf_op jit(solution)/shard_map/dot_general | solution.py:602
  11.2 0.0 copy-done.6
  11.2 1.5 %convolution_convert_fusion.refs_7_ = bf16[768,512]{1,0:T(8,128)(2,1)} fusion(bf16[768,512]{1,0:T(8,128)(2,1)S(1)} %get-tuple-element.66.act_ref, bf16[512,512]{1,0:T(8,128)(2,1)S(1)} %copy-done.6), kind=kOutput, calls=%fused_computation.16 | convolution fusion | flops 403046400 | bytes 2097152 | tf_op jit(solution)/shard_map/dot_general | solution.py:606
  12.6 0.9 copy-done.3
  13.5 0.0 copy-done
  13.5 0.0 copy-done.7
  13.5 0.1 fusion
  13.6 0.0 collective-permute-done.1
  13.6 0.0 collective-permute-done
  13.6 1.4 %pack_columns.1 = (f32[5,56,128]{2,1,0:T(8,128)S(1)}, f32[5,56,128]{2,1,0:T(8,128)S(1)}) custom-call(f32[3072,128]{1,0:T(8,128)S(1)} %bitcast.17, f32[64,128]{1,0:T(8,128)S(1)} %copy-done.7, f32[392,128]{1,0:T(8,128)S(1)} %bitcast.27, f32[392,128]{1,0:T(8,128)S(1)} %bitcast.23), custom_call_target="tpu_custom_call" | custom-call | tf_op jit(solution)/shard_map/pack_columns/pallas_call | solution.py:537
  15.1 0.1 pad_maximum_fusion.1
  15.2 0.0 copy-start.5
  15.2 0.3 constant_dynamic-slice_fusion
  15.5 0.0 copy-start.11
  15.5 0.0 copy-start.12
  15.5 4.0 %collective-permute-start.5 = (f32[5,56,128]{2,1,0:T(8,128)S(1)}, f32[5,56,128]{2,1,0:T(8,128)S(1)}, u32[]{:S(2)}, u32[]{:S(2)}) collective-permute-start(f32[5,56,128]{2,1,0:T(8,128)S(1)} %get-tuple-element.42), channel_id=1, source_target_pairs={{0,1},{1,2},{2,3},{4,5},{5,6},{6,7},{8,9},{9,10},{10,11},{12,13},{... | collective-permute-start | bytes 430088 | tf_op jit(solution)/shard_map/ppermute | solution.py:25
  19.6 1.3 %collective-permute-start.6 = (f32[5,56,128]{2,1,0:T(8,128)S(1)}, f32[5,56,128]{2,1,0:T(8,128)S(1)}, u32[]{:S(2)}, u32[]{:S(2)}) collective-permute-start(f32[5,56,128]{2,1,0:T(8,128)S(1)} %get-tuple-element.43), channel_id=1, source_target_pairs={{1,0},{2,1},{3,2},{5,4},{6,5},{7,6},{9,8},{10,9},{11,10},{13,12},{... | collective-permute-start | bytes 430088 | tf_op jit(solution)/shard_map/ppermute | solution.py:25
  20.9 2.7 %collective-permute-start.2 = (bf16[49,32,128]{2,1,0:T(8,128)(2,1)S(1)}, bf16[49,32,128]{2,1,0:T(8,128)(2,1)S(1)}, u32[]{:S(2)}, u32[]{:S(2)}) collective-permute-start(bf16[49,32,128]{2,1,0:T(8,128)(2,1)S(1)} %get-tuple-element.37), channel_id=1, source_target_pairs={{0,1},{1,2},{2,3},{3,0},{4,5},{5,6},{6,7},{7,4},{8,9},{9,10},{10,1... | collective-permute-start | bytes 1204232 | tf_op jit(solution)/shard_map/ppermute | solution.py:551
  23.6 2.6 %collective-permute-start.3 = (bf16[49,32,128]{2,1,0:T(8,128)(2,1)S(1)}, bf16[49,32,128]{2,1,0:T(8,128)(2,1)S(1)}, u32[]{:S(2)}, u32[]{:S(2)}) collective-permute-start(bf16[49,32,128]{2,1,0:T(8,128)(2,1)S(1)} %get-tuple-element.38), channel_id=1, source_target_pairs={{0,2},{1,3},{2,0},{3,1},{4,6},{5,7},{6,4},{7,5},{8,10},{9,11},{10,... | collective-permute-start | bytes 1204232 | tf_op jit(solution)/shard_map/ppermute | solution.py:551
  26.1 1.3 %collective-permute-start.4 = (bf16[49,32,128]{2,1,0:T(8,128)(2,1)S(1)}, bf16[49,32,128]{2,1,0:T(8,128)(2,1)S(1)}, u32[]{:S(2)}, u32[]{:S(2)}) collective-permute-start(bf16[49,32,128]{2,1,0:T(8,128)(2,1)S(1)} %get-tuple-element.39), channel_id=1, source_target_pairs={{0,3},{1,0},{2,1},{3,2},{4,7},{5,4},{6,5},{7,6},{8,11},{9,8},{10,9... | collective-permute-start | bytes 1204232 | tf_op jit(solution)/shard_map/ppermute | solution.py:551
  27.5 0.0 copy-done.5
  27.5 3.4 %copy-done.13 = bf16[512,16,512]{2,1,0:T(8,128)(2,1)S(1)} copy-done((bf16[512,16,512]{2,1,0:T(8,128)(2,1)S(1)}, bf16[512,16,512]{2,1,0:T(8,128)(2,1)}, u32[]{:S(2)}) %copy-start.13) | copy-done | bytes 8388632
  30.9 11.2 %decoder_order.1.refs_8_ = bf16[512,8192]{1,0:T(8,128)(2,1)S(1)} custom-call(bf16[512,16,512]{2,1,0:T(8,128)(2,1)S(1)} %copy-done.13, bf16[512,512]{1,0:T(8,128)(2,1)S(1)} %copy-done.5), custom_call_target="tpu_custom_call" | custom-call | flops 10000000000 | bytes 10000000 | tf_op jit(solution)/shard_map/decoder_order/pallas_call | solution.py:554
  42.1 0.0 collective-permute-done.5.refs_4_
  42.1 0.0 collective-permute-done.6.refs_5_
  42.1 0.0 copy-done.11
  42.1 0.0 copy-done.12
  42.1 0.0 copy-done.18
  42.1 0.0 copy-done.20
  42.1 0.0 copy-start.16
  42.2 9.1 %tile_solver.3.refs_10_ = f32[3072,128]{1,0:T(8,128)} custom-call(f32[3072,128]{1,0:T(8,128)S(1)} %bitcast.18, f32[64,128]{1,0:T(8,128)S(1)} %copy-done.7, f32[392,128]{1,0:T(8,128)S(1)} %bitcast.28, f32[392,128]{1,0:T(8,128)S(1)} %bitcast.24, f32[5,56,128]{2,1,0:T(8,128)S(1)} %collective-permute-done.5.refs_4_, ...), custom_call_target="tpu_custom_call" | custom-call | flops 99999997952 | bytes 10000000 | tf_op jit(solution)/shard_map/tile_solver/pallas_call | solution.py:571
  51.3 9.1 %tile_solver.4.refs_10_ = f32[3072,128]{1,0:T(8,128)} custom-call(f32[3072,128]{1,0:T(8,128)S(1)} %bitcast.19, f32[64,128]{1,0:T(8,128)S(1)} %copy-done.7, f32[392,128]{1,0:T(8,128)S(1)} %bitcast.29, f32[392,128]{1,0:T(8,128)S(1)} %bitcast.25, f32[5,56,128]{2,1,0:T(8,128)S(1)} %collective-permute-done.5.refs_4_, ...), custom_call_target="tpu_custom_call", output_to_operand_aliasing={{}: (10, {})} | custom-call | flops 10000000000 | bytes 10000000 | tf_op jit(solution)/shard_map/tile_solver/pallas_call | solution.py:571
  60.4 0.0 collective-permute-done.2.refs_1_
  60.4 0.0 collective-permute-done.3.refs_2_
  60.4 0.0 collective-permute-done.4.refs_3_
  60.5 22.1 %strip_solver.1 = (bf16[384,512]{1,0:T(8,128)(2,1)S(1)}, f32[1,512]{1,0:T(1,128)S(1)}) custom-call(bf16[49,32,128]{2,1,0:T(8,128)(2,1)S(1)} %get-tuple-element.36.refs_0_, bf16[49,32,128]{2,1,0:T(8,128)(2,1)S(1)} %collective-permute-done.2.refs_1_, bf16[49,32,128]{2,1,0:T(8,128)(2,1)S(1)} %collective-permute-done.3.refs_2_, ...), custom_call_target="tpu_custom_call" | custom-call | tf_op jit(solution)/shard_map/strip_solver/pallas_call | solution.py:609
  82.6 19.4 %all_to_all.10.pieces_ref = bf16[16,24,512]{2,1,0:T(8,128)(2,1)S(1)} all-to-all(bf16[16,24,512]{2,1,0:T(8,128)(2,1)S(1)} %bitcast.31), channel_id=1, replica_groups=mesh['run'=2,'row'=4,'col'=4] {'row','col'}, dimensions={0} | all-to-all | bytes 786432 | tf_op jit(solution)/shard_map/all_to_all | solution.py:638
  102.0 0.9 share_sum.1
  102.9 3.8 %all-to-all-start.1 = ((bf16[16,32,512]{2,1,0:T(8,128)(2,1)}), bf16[16,32,512]{2,1,0:T(8,128)(2,1)S(1)}, u32[]{:S(2)}, u32[]{:S(2)}) async-start(bf16[16,32,512]{2,1,0:T(8,128)(2,1)} %share_sum.1), calls=%async_computation.1 | async-start | bytes 1048576 | tf_op jit(solution)/shard_map/all_to_all | solution.py:655
  106.7 0.9 copy-done.15
  107.6 0.9 copy-done.17
  108.5 1.7 %copy-done.19 = bf16[1024,1152]{1,0:T(8,128)(2,1)S(1)} copy-done((bf16[1024,1152]{1,0:T(8,128)(2,1)S(1)}, bf16[1024,1152]{1,0:T(8,128)(2,1)}, u32[]{:S(2)}) %copy-start.19) | copy-done | bytes 2359320
  110.2 1.3 copy-done.21
  111.5 9.1 %tile_solver.5 = f32[3072,128]{1,0:T(8,128)} custom-call(f32[3072,128]{1,0:T(8,128)S(1)} %bitcast.20, f32[64,128]{1,0:T(8,128)S(1)} %copy-done.7, f32[392,128]{1,0:T(8,128)S(1)} %bitcast.30, f32[392,128]{1,0:T(8,128)S(1)} %bitcast.26, f32[5,56,128]{2,1,0:T(8,128)S(1)} %copy-done.15, f32[5,56,128]{2,1,0:T(8,128)S(1)} %copy-done.17, ...), custom_call_target="tpu_custom_call", output_to_operand_aliasing={{}: (10, {})} | custom-call | flops 10000000000 | bytes 10000000 | tf_op jit(solution)/shard_map/tile_solver/pallas_call | solution.py:571
  120.6 0.0 all-to-all-done.1.mine_ref
  120.6 0.0 collective-permute-start.7
  120.6 1.9 %collective-permute-done.7.other_ref = bf16[16,32,512]{2,1,0:T(8,128)(2,1)S(1)} collective-permute-done((bf16[16,32,512]{2,1,0:T(8,128)(2,1)S(1)}, bf16[16,32,512]{2,1,0:T(8,128)(2,1)S(1)}, u32[]{:S(2)}, u32[]{:S(2)}) %collective-permute-start.7) | collective-permute-done | bytes 524320 | tf_op jit(solution)/shard_map/ppermute | solution.py:658
  122.5 1.4 %copy-done.1 = f32[768,512]{1,0:T(8,128)S(1)} copy-done((f32[768,512]{1,0:T(8,128)S(1)}, f32[768,512]{1,0:T(8,128)}, u32[]{:S(2)}) %copy-start.1) | copy-done | bytes 1572888
  123.9 1.1 copy-done.4
  125.1 0.9 copy-done.9
  126.0 2.3 %trunk_update.1 = (f32[256,512]{1,0:T(8,128)}, f32[1,512]{1,0:T(1,128)}, f32[512,512]{1,0:T(8,128)}, f32[1,128]{1,0:T(1,128)}) custom-call(bf16[16,32,512]{2,1,0:T(8,128)(2,1)S(1)} %all-to-all-done.1.mine_ref, bf16[16,32,512]{2,1,0:T(8,128)(2,1)S(1)} %collective-permute-done.7.other_ref, bf16[768,512]{1,0:T(8,128)(2,1)S(1)} %copy-done.4, ...), custom_call_target="tpu_custom_call" | custom-call | tf_op jit(solution)/shard_map/trunk_update/pallas_call | solution.py:660
  (22 shorter events, 0.1 us)
Async XLA Ops:
  0.6 7.9 %copy-start.23 = (bf16[8,256]{1,0:T(8,128)(2,1)S(1)}, bf16[8,256]{1,0:T(8,128)(2,1)}, u32[]{:S(2)}) copy-start(bf16[8,256]{1,0:T(8,128)(2,1)} %param.18) | copy-start | bytes 12292
  0.6 8.0 %copy-start.22 = (bf16[96,256]{1,0:T(8,128)(2,1)S(1)}, bf16[96,256]{1,0:T(8,128)(2,1)}, u32[]{:S(2)}) copy-start(bf16[96,256]{1,0:T(8,128)(2,1)} %param.17) | copy-start | bytes 147460
  0.7 8.1 %copy-start.10 = (f32[512]{0:T(512)S(1)}, f32[512]{0:T(512)}, u32[]{:S(2)}) copy-start(f32[512]{0:T(512)} %param.20) | copy-start | bytes 6148
  0.7 8.1 %copy-start.8 = (bf16[256,512]{1,0:T(8,128)(2,1)S(1)}, bf16[256,512]{1,0:T(8,128)(2,1)}, u32[]{:S(2)}) copy-start(bf16[256,512]{1,0:T(8,128)(2,1)} %w_in_ref.1) | copy-start | bytes 786436
  1.8 11.8 %collective-permute-start.1 = (f32[49,8,128]{2,1,0:T(8,128)S(1)}, f32[49,8,128]{2,1,0:T(8,128)S(1)}, u32[]{:S(2)}, u32[]{:S(2)}) collective-permute-start(f32[49,8,128]{2,1,0:T(8,128)S(1)} %get-tuple-element.63), channel_id=1, source_target_pairs={{4,0},{8,4},{12,8},{5,1},{9,5},{13,9},{6,2},{10,6},{14,10},{7,3},{... | collective-permute-start | bytes 602120 | tf_op jit(solution)/shard_map/ppermute | solution.py:25
  3.1 10.5 %collective-permute-start = (f32[49,8,128]{2,1,0:T(8,128)S(1)}, f32[49,8,128]{2,1,0:T(8,128)S(1)}, u32[]{:S(2)}, u32[]{:S(2)}) collective-permute-start(f32[49,8,128]{2,1,0:T(8,128)S(1)} %get-tuple-element.64), channel_id=1, source_target_pairs={{0,4},{4,8},{8,12},{1,5},{5,9},{9,13},{2,6},{6,10},{10,14},{3,7},{... | collective-permute-start | bytes 602120 | tf_op jit(solution)/shard_map/ppermute | solution.py:25
  8.7 2.5 %copy-start.6 = (bf16[512,512]{1,0:T(8,128)(2,1)S(1)}, bf16[512,512]{1,0:T(8,128)(2,1)}, u32[]{:S(2)}) copy-start(bf16[512,512]{1,0:T(8,128)(2,1)} %w_out_ref.1) | copy-start | bytes 1572868
  11.2 2.3 %copy-start = (f32[48,64,128]{2,1,0:T(8,128)S(1)}, f32[48,64,128]{2,1,0:T(8,128)}, u32[]{:S(2)}) copy-start(f32[48,64,128]{2,1,0:T(8,128)} %param.13) | copy-start | bytes 4718596
  11.2 2.3 %copy-start.7 = (f32[64,128]{1,0:T(8,128)S(1)}, f32[64,128]{1,0:T(8,128)}, u32[]{:S(2)}) copy-start(f32[64,128]{1,0:T(8,128)} %refs_1_.5) | copy-start | bytes 98308
  12.6 0.9 copy-start.3
  15.2 12.3 %copy-start.5 = (bf16[512,512]{1,0:T(8,128)(2,1)S(1)}, bf16[512,512]{1,0:T(8,128)(2,1)}, u32[]{:S(2)}) copy-start(bf16[512,512]{1,0:T(8,128)(2,1)} %constant.57.clone.order_ref.refs_4_) | copy-start | bytes 1572868
  15.5 26.6 %copy-start.11 = (f32[48]{0:T(128)S(1)}, f32[48]{0:T(128)}, u32[]{:S(2)}) copy-start(f32[48]{0:T(128)} %refs_6_.7) | copy-start | bytes 580
  15.5 26.6 %copy-start.12 = (s32[48]{0:T(128)S(1)}, s32[48]{0:T(128)}, u32[]{:S(2)}) copy-start(s32[48]{0:T(128)} %refs_7_.5) | copy-start | bytes 580
  15.5 26.5 %collective-permute-start.5 = (f32[5,56,128]{2,1,0:T(8,128)S(1)}, f32[5,56,128]{2,1,0:T(8,128)S(1)}, u32[]{:S(2)}, u32[]{:S(2)}) collective-permute-start(f32[5,56,128]{2,1,0:T(8,128)S(1)} %get-tuple-element.42), channel_id=1, source_target_pairs={{0,1},{1,2},{2,3},{4,5},{5,6},{6,7},{8,9},{9,10},{10,11},{12,13},{... | collective-permute-start | bytes 430088 | tf_op jit(solution)/shard_map/ppermute | solution.py:25
  19.6 22.5 %collective-permute-start.6 = (f32[5,56,128]{2,1,0:T(8,128)S(1)}, f32[5,56,128]{2,1,0:T(8,128)S(1)}, u32[]{:S(2)}, u32[]{:S(2)}) collective-permute-start(f32[5,56,128]{2,1,0:T(8,128)S(1)} %get-tuple-element.43), channel_id=1, source_target_pairs={{1,0},{2,1},{3,2},{5,4},{6,5},{7,6},{9,8},{10,9},{11,10},{13,12},{... | collective-permute-start | bytes 430088 | tf_op jit(solution)/shard_map/ppermute | solution.py:25
  20.9 39.6 %collective-permute-start.2 = (bf16[49,32,128]{2,1,0:T(8,128)(2,1)S(1)}, bf16[49,32,128]{2,1,0:T(8,128)(2,1)S(1)}, u32[]{:S(2)}, u32[]{:S(2)}) collective-permute-start(bf16[49,32,128]{2,1,0:T(8,128)(2,1)S(1)} %get-tuple-element.37), channel_id=1, source_target_pairs={{0,1},{1,2},{2,3},{3,0},{4,5},{5,6},{6,7},{7,4},{8,9},{9,10},{10,1... | collective-permute-start | bytes 1204232 | tf_op jit(solution)/shard_map/ppermute | solution.py:551
  23.6 36.9 %collective-permute-start.3 = (bf16[49,32,128]{2,1,0:T(8,128)(2,1)S(1)}, bf16[49,32,128]{2,1,0:T(8,128)(2,1)S(1)}, u32[]{:S(2)}, u32[]{:S(2)}) collective-permute-start(bf16[49,32,128]{2,1,0:T(8,128)(2,1)S(1)} %get-tuple-element.38), channel_id=1, source_target_pairs={{0,2},{1,3},{2,0},{3,1},{4,6},{5,7},{6,4},{7,5},{8,10},{9,11},{10,... | collective-permute-start | bytes 1204232 | tf_op jit(solution)/shard_map/ppermute | solution.py:551
  26.1 34.3 %collective-permute-start.4 = (bf16[49,32,128]{2,1,0:T(8,128)(2,1)S(1)}, bf16[49,32,128]{2,1,0:T(8,128)(2,1)S(1)}, u32[]{:S(2)}, u32[]{:S(2)}) collective-permute-start(bf16[49,32,128]{2,1,0:T(8,128)(2,1)S(1)} %get-tuple-element.39), channel_id=1, source_target_pairs={{0,3},{1,0},{2,1},{3,2},{4,7},{5,4},{6,5},{7,6},{8,11},{9,8},{10,9... | collective-permute-start | bytes 1204232 | tf_op jit(solution)/shard_map/ppermute | solution.py:551
  27.5 3.4 %copy-start.13 = (bf16[512,16,512]{2,1,0:T(8,128)(2,1)S(1)}, bf16[512,16,512]{2,1,0:T(8,128)(2,1)}, u32[]{:S(2)}) copy-start(bf16[512,16,512]{2,1,0:T(8,128)(2,1)} %d_ref.1) | copy-start | bytes 25165828
  30.9 11.3 %copy-start.18 = (bf16[1024,1152]{1,0:T(8,128)(2,1)S(1)}, bf16[1024,1152]{1,0:T(8,128)(2,1)}, u32[]{:S(2)}) copy-start(bf16[1024,1152]{1,0:T(8,128)(2,1)} %constant.58.clone.refs_8_) | copy-start | bytes 7077892
  30.9 11.3 %copy-start.20 = (bf16[2,256,1152]{2,1,0:T(8,128)(2,1)S(1)}, bf16[2,256,1152]{2,1,0:T(8,128)(2,1)}, u32[]{:S(2)}) copy-start(bf16[2,256,1152]{2,1,0:T(8,128)(2,1)} %constant.59.clone.refs_9_) | copy-start | bytes 3538948
  42.1 9.2 %copy-start.14 = (f32[5,56,128]{2,1,0:T(8,128)}, f32[5,56,128]{2,1,0:T(8,128)S(1)}, u32[]{:S(2)}) copy-start(f32[5,56,128]{2,1,0:T(8,128)S(1)} %collective-permute-done.5.refs_4_) | copy-start | bytes 430084
  42.1 9.2 %copy-start.16 = (f32[5,56,128]{2,1,0:T(8,128)}, f32[5,56,128]{2,1,0:T(8,128)S(1)}, u32[]{:S(2)}) copy-start(f32[5,56,128]{2,1,0:T(8,128)S(1)} %collective-permute-done.6.refs_5_) | copy-start | bytes 430084
  51.3 9.2 %copy-start.2 = (bf16[768,512]{1,0:T(8,128)(2,1)S(1)}, bf16[768,512]{1,0:T(8,128)(2,1)}, u32[]{:S(2)}) copy-start(bf16[768,512]{1,0:T(8,128)(2,1)} %convolution_convert_fusion.refs_7_) | copy-start | bytes 2359300
  102.9 17.7 %all-to-all-start.1 = ((bf16[16,32,512]{2,1,0:T(8,128)(2,1)}), bf16[16,32,512]{2,1,0:T(8,128)(2,1)S(1)}, u32[]{:S(2)}, u32[]{:S(2)}) async-start(bf16[16,32,512]{2,1,0:T(8,128)(2,1)} %share_sum.1), calls=%async_computation.1 | async-start | bytes 1048576 | tf_op jit(solution)/shard_map/all_to_all | solution.py:655
  106.7 0.9 copy-start.15
  107.6 0.9 copy-start.17
  108.5 1.7 %copy-start.19 = (bf16[1024,1152]{1,0:T(8,128)(2,1)S(1)}, bf16[1024,1152]{1,0:T(8,128)(2,1)}, u32[]{:S(2)}) copy-start(bf16[1024,1152]{1,0:T(8,128)(2,1)} %constant.58.clone.refs_8_) | copy-start | bytes 7077892
  110.2 1.3 copy-start.21
  120.6 1.9 %collective-permute-start.7 = (bf16[16,32,512]{2,1,0:T(8,128)(2,1)S(1)}, bf16[16,32,512]{2,1,0:T(8,128)(2,1)S(1)}, u32[]{:S(2)}, u32[]{:S(2)}) collective-permute-start(bf16[16,32,512]{2,1,0:T(8,128)(2,1)S(1)} %all-to-all-done.1.mine_ref), channel_id=1, source_target_pairs={{0,16},{16,0},{1,17},{17,1},{2,18},{18,2},{3,19},{19,3},{4,20},{20... | collective-permute-start | bytes 1572872 | tf_op jit(solution)/shard_map/ppermute | solution.py:658
  122.5 1.4 %copy-start.1 = (f32[768,512]{1,0:T(8,128)S(1)}, f32[768,512]{1,0:T(8,128)}, u32[]{:S(2)}) copy-start(f32[768,512]{1,0:T(8,128)} %get-tuple-element.58.slope_ref) | copy-start | bytes 4718596
  123.9 1.1 copy-start.4
  125.1 0.9 copy-start.9

commit v3 on v2

--- a/solution.py
+++ b/solution.py
@@ -1,4 +1,5 @@
 import functools
+import math
 
 import jax
 import jax.numpy as jnp
@@ -98,7 +99,7 @@
         & (source % half // halo == seg_row)
         & (source % halo + high * (cols_dev + halo) == column)
     )
-    return jnp.asarray(main, bf16), jnp.asarray(edge.reshape(2, 2 * LANES, -1), bf16)
+    return jnp.asarray(np.concatenate([main, edge.reshape(4 * LANES, -1)]), bf16)
 
 
 def row_source(halo, rows_dev, runs, refs):
@@ -162,12 +163,13 @@
 
 def tile_kernel(part, halo, steps, runs, *refs):
     x_ref, cond_ref, top_ref, bottom_ref, left_ref, right_ref, nonlin_ref, counts_ref = refs[:8]
-    main_ref, edge_ref = refs[8:10]
+    places_ref = refs[8]
     out_ref, u_ref, c_ref, rate_ref, body_ref, ends_ref, back_ref, pad_ref = refs[-8:]
     rows_dev, cols_dev = cond_ref.shape
     deep = (rows_dev + 2 * halo) // ROW_SEGS
     across = (cols_dev + 2 * halo) // COL_SEGS
     packs = left_ref.shape[0]
+    edges = ROW_SEGS * cols_dev
     first_run = part * GROUP
     row_at, row_count = lax.axis_index("row"), lax.axis_size("row")
     col_at, col_count = lax.axis_index("col"), lax.axis_size("col")
@@ -208,10 +210,10 @@
         total = None
         extra = [None, None]
         for i in range(PIECES):
-            more = jnp.dot(body_ref[i], main_ref[:, lanes], preferred_element_type=f32)
+            more = jnp.dot(body_ref[i], places_ref[:edges, lanes], preferred_element_type=f32)
             total = more if total is None else total + more
             for parity in range(2):
-                more = jnp.dot(ends_ref[i], edge_ref[parity, :, lanes], preferred_element_type=f32)
+                more = jnp.dot(ends_ref[i], places_ref[edges + 2 * LANES * parity : edges + 2 * LANES * (parity + 1), lanes], preferred_element_type=f32)
                 extra[parity] = more if extra[parity] is None else extra[parity] + more
         for b in range(deep):
             first = b // 2 * GROUP
@@ -292,7 +294,7 @@
         total = None
         for i in range(PIECES):
             more = lax.dot_general(
-                back_ref[i], main_ref[places, :], (((1,), (1,)), ((), ())), preferred_element_type=f32
+                back_ref[i], places_ref[places, :], (((1,), (1,)), ((), ())), preferred_element_type=f32
             )
             total = more if total is None else total + more
         for b in range(deep):
@@ -420,19 +422,24 @@
         for row in range(halo + band, rows - 1 - number):
             carry = one(row, carry, bottom_scale, False)
         square_ref[...] += carry[3]
+        half = gram_ref.shape[0] // 2
         for spare in range(each * number // steps, each * (number + 1) // steps):
             lanes = pl.ds(pl.multiple_of((index * each + spare) * wide, wide), wide)
             cell = weights_ref[:, lanes]
-            gram_ref[...] += lax.dot_general(
-                cell, cell, (((1,), (1,)), ((), ())), preferred_element_type=f32
+            dims = (((1,), (1,)), ((), ()))
+            gram_ref[:half] += lax.dot_general(cell[:half], cell, dims, preferred_element_type=f32)
+            gram_ref[half:, half:] += lax.dot_general(
+                cell[half:], cell[half:], dims, preferred_element_type=f32
             )
 
     @pl.when(index == pl.num_programs(0) - 1)
     def _():
         size = runs * steps
         hidden = hidden_ref[pl.ds(pl.multiple_of(lax.axis_index("run") * size, size), size), :]
+        half = gram_ref.shape[0] // 2
+        lower = jnp.concatenate([gram_ref[:half, half:].T, gram_ref[half:, half:]], axis=1)
         pushed = None
-        for piece in pieces_of(gram_ref[...]):
+        for piece in pieces_of(jnp.concatenate([gram_ref[:half], lower], axis=0)):
             part = jnp.dot(hidden, piece, preferred_element_type=f32)
             pushed = part if pushed is None else pushed + part
         drawn = product(shot_ref, weights_ref)
@@ -454,9 +461,16 @@
 
 
 def finish_kernel(
-    share, loss_scale, mine_ref, other_ref, act_ref, slope_ref, rows_ref, w_in_ref, bias_ref,
+    share, loss_scale, mine_ref, other_ref, rows_ref, w_in_ref, bias_ref,
     w_out_ref, new_in_ref, new_bias_ref, new_out_ref, loss_ref, grad_ref, parts_ref,
 ):
+    pre = jnp.dot(rows_ref[...], w_in_ref[...], preferred_element_type=f32) + bias_ref[...]
+    root, cube = (2.0 / math.pi) ** 0.5, 0.044715
+    square = pre * pre
+    bend = jnp.tanh(root * pre * (1.0 + cube * square))
+    rise = 0.5 + 0.5 * bend
+    act = (pre * rise).astype(bf16)
+    slope = rise + 0.5 * pre * (1.0 - bend * bend) * (root * (1.0 + 3.0 * cube * square))
     core = lax.axis_index("run")
     cells = mine_ref.shape[0]
     for at, ref in ((core, mine_ref), (1 - core, other_ref)):
@@ -476,12 +490,12 @@
     loss_ref[...] = jnp.broadcast_to(loss, loss_ref.shape)
     grad = grad_ref[...]
     by_rows = (((0,), (0,)), ((), ()))
-    grad_out = lax.dot_general(act_ref[...], grad, by_rows, preferred_element_type=f32)
+    grad_out = lax.dot_general(act, grad, by_rows, preferred_element_type=f32)
     new_out_ref[...] = w_out_ref[...].astype(f32) - learn_rate * grad_out
     back = lax.dot_general(
         grad, w_out_ref[...], (((1,), (1,)), ((), ())), preferred_element_type=f32
     )
-    grad_pre = back * slope_ref[...]
+    grad_pre = back * slope
     new_bias_ref[...] = bias_ref[...] - learn_rate * jnp.sum(grad_pre, axis=0, keepdims=True)
     grad_in = lax.dot_general(
         rows_ref[...], grad_pre.astype(bf16), by_rows, preferred_element_type=f32
@@ -550,7 +564,7 @@
         pairs = [(i, (i + hop) % col_size) for i in range(col_size)]
         blocks.append(lax.ppermute(messages[hop], "col", pairs))
 
-    size = 64
+    size = 128
     weights = pl.pallas_call(
         decoder_kernel,
         grid=(hidden_size // size,),
@@ -558,12 +572,12 @@
         in_specs=[pl.BlockSpec((size, band, wide), lambda i: (i, 0, 0)), in_vmem],
         out_specs=pl.BlockSpec((size, band * wide), lambda i: (i, 0)),
         scratch_shapes=[pltpu.VMEM((wide // LANES, size * band, LANES), f32)],
-        compiler_params=vmem(12),
+        compiler_params=vmem(20),
         cost_estimate=pl.CostEstimate(flops=10**10, bytes_accessed=10**7, transcendentals=0),
         name="decoder_order",
     )(decoder, order)
 
-    main, edge = tile_order(halo, cols_dev)
+    places = tile_order(halo, cols_dev)
 
     def solve(part, left, right, done):
         block = pl.BlockSpec((GROUP * rows_dev, cols_dev), lambda i: (part, 0))
@@ -572,7 +586,7 @@
             functools.partial(tile_kernel, part, halo, steps, runs),
             grid=(1,),
             out_shape=jax.ShapeDtypeStruct((runs * rows_dev, cols_dev), f32),
-            in_specs=[block] + [in_vmem] * 5 + [in_smem] * 2 + [in_vmem] * 2 + [in_hbm] * len(done),
+            in_specs=[block] + [in_vmem] * 5 + [in_smem] * 2 + [in_vmem] + [in_hbm] * len(done),
             out_specs=block,
             scratch_shapes=[
                 pltpu.VMEM((2, deep, across, GROUP, LANES), f32),
@@ -583,13 +597,13 @@
                 pltpu.VMEM((PIECES, deep * GROUP, across * LANES), bf16),
                 pltpu.VMEM((rows_dev + 2 * halo + COND_ROWS, cols_dev), f32),
             ],
-            input_output_aliases={10: 0} if done else {},
+            input_output_aliases={9: 0} if done else {},
             compiler_params=vmem(14),
             cost_estimate=pl.CostEstimate(
                 flops=10**10 if done else 10**11, bytes_accessed=10**7, transcendentals=0
             ),
             name="tile_solver",
-        )(*tile_args, left, right, nonlin, counts, main, edge, *done)
+        )(*tile_args, left, right, nonlin, counts, places, *done)
 
     early = FRONT_PARTS
     field = ()
@@ -600,11 +614,8 @@
     codes = time_code.astype(f32)[None, :, None, :]
     rows_in = (desc + codes).astype(bf16).reshape(rows_all, -1)
     pre = jnp.dot(rows_in, w_in, preferred_element_type=f32) + bias_in
-    act, pull = jax.vjp(jax.nn.gelu, pre)
-    slope = pull(jnp.ones_like(pre))[0]
-    act = act.astype(bf16)
+    act = jax.nn.gelu(pre).astype(bf16)
     hidden = jnp.dot(act, w_out, preferred_element_type=f32).astype(bf16)
-    hidden, slope = lax.optimization_barrier((hidden, slope))
     hidden, *field = lax.optimization_barrier((hidden, *field))
     partial, loss = pl.pallas_call(
         functools.partial(strip_kernel, halo, steps, runs, scale_of),
@@ -665,15 +676,15 @@
             jax.ShapeDtypeStruct((hidden_size, hidden_size), f32),
             jax.ShapeDtypeStruct((1, LANES), f32),
         ),
-        in_specs=[in_vmem] * 8,
+        in_specs=[in_vmem] * 6,
         out_specs=(in_vmem,) * 4,
         scratch_shapes=[
             pltpu.VMEM((rows_all, hidden_size), bf16),
             pltpu.VMEM((run_size, hidden_size), f32),
         ],
-        compiler_params=vmem(12),
+        compiler_params=vmem(20),
         name="trunk_update",
-    )(gathered, other, act, slope, rows_in, w_in, bias_in[None], w_out)
+    )(gathered, other, rows_in, w_in, bias_in[None], w_out)
     return (final_field, new_w_in, new_bias[0], new_w_out, mean_loss[0, 0])
 
 

time: 129 us -> 127 us (0.984)
  local copies, waits for them, and re-layouts: 12.8 us -> 5.13 us
  blocking collectives: 19.4 us -> 24 us
  waiting for transfers between devices: 1.93 us -> 4.28 us
  matrix products: 3.89 us -> 1.89 us
    unnamed x48 -> x38, local copies, waits for them, and re-layouts: 12.6 us -> 4.84 us
    all_to_all x1, blocking collectives: 19.4 us -> 24 us  [per_device(): lax.all_to_all(partial.reshape(cells, share, hidden_size), ('row', 'col')...]
    dot_general x1 -> x0, matrix products: 2.44 us -> none  [per_device(): pre = jnp.dot(rows_in, w_in, preferred_element_type=f32) + bias_in]
    ppermute x4, waiting for transfers between devices: 0.01 us -> 2.36 us  [neighbours(): return (lax.ppermute(up, axis, forward), lax.ppermute(down, axis, backward))]
  transfers between devices with their start and end apart: 9 -> 9, of which waited for: 1 -> 3; matrix products, arithmetic and copies ran while one was open for 3% -> 2% of each run, Pallas kernels for 30% -> 30%
where the time goes in v3:
time: 127 us; the launch traced here: 126 us
  Pallas kernels  65.4 us (51%)
  blocking collectives  24 us (19%)
  starting transfers between devices  22.5 us (18%)
  local copies, waits for them, and re-layouts  5.13 us (4%)
  waiting for transfers between devices  4.28 us (3%)
  other arithmetic  2.16 us (2%)
  matrix products  1.89 us (1%)
    pallas_call x3, Pallas kernels, solve(): pl.pallas_call(functools.partial(tile_kernel, part, halo, steps, runs), g...  27.4 us
    all_to_all x1, blocking collectives, per_device(): lax.all_to_all(partial.reshape(cells, share, hidden_size), ('row', 'col')...  24 us
    pallas_call x1, Pallas kernels, per_device(): pl.pallas_call(functools.partial(strip_kernel, halo, steps, runs, scale_o...  21.6 us
    ppermute x4, starting transfers between devices, neighbours(): return (lax.ppermute(up, axis, forward), lax.ppermute(down, axis, backward))  12 us
    pallas_call x1, Pallas kernels, per_device(): pl.pallas_call(decoder_kernel, grid=(hidden_size // size,), out_shape=jax...  11 us
    ppermute x3, starting transfers between devices, per_device(): blocks.append(lax.ppermute(messages[hop], 'col', pairs))  6.63 us
    unnamed x38, local copies, waits for them, and re-layouts  4.84 us
    all_to_all x1, starting transfers between devices, per_device(): gathered = lax.all_to_all(message_out, ('row', 'col'), 0, 0, tiled=True)  3.83 us
  transfers between devices with their start and end apart: 9, of which 3 were waited for; matrix products, arithmetic and copies ran while one was open for 2% of the time, Pallas kernels for 30%

profile of v3, /device:TPU:0, one launch (start us, length us, event | category | flops | bytes accessed | tf_op | source)
XLA Modules:
  0.0 126.3 jit_solution(18307405639289868819)
XLA Ops:
  0.6 0.0 copy-start.18
  0.6 0.0 copy-start.17
  0.7 0.0 copy-start.2
  0.7 0.0 copy-start.7
  0.7 0.0 copy-start.5
  0.7 1.9 %fusion.15 = (f32[49,8,128]{2,1,0:T(8,128)}, f32[49,8,128]{2,1,0:T(8,128)}) fusion(f32[48,64,128]{2,1,0:T(8,128)} %param.12, f32[1,64,128]{2,1,0:T(8,128)} %bitcast.31), kind=kLoop, calls=%fused_computation.24 | loop fusion | flops 100352 | bytes 2007040 | tf_op jit(solution)/shard_map/concatenate | solution.py:531
  2.6 1.3 %collective-permute-start.1 = (f32[49,8,128]{2,1,0:T(8,128)}, f32[49,8,128]{2,1,0:T(8,128)S(1)}, u32[]{:S(2)}, u32[]{:S(2)}) collective-permute-start(f32[49,8,128]{2,1,0:T(8,128)} %get-tuple-element.59), channel_id=1, source_target_pairs={{4,0},{8,4},{12,8},{5,1},{9,5},{13,9},{6,2},{10,6},{14,10},{7,3},{... | collective-permute-start | bytes 602120 | tf_op jit(solution)/shard_map/ppermute | solution.py:26
  3.8 5.5 %collective-permute-start = (f32[49,8,128]{2,1,0:T(8,128)}, f32[49,8,128]{2,1,0:T(8,128)S(1)}, u32[]{:S(2)}, u32[]{:S(2)}) collective-permute-start(f32[49,8,128]{2,1,0:T(8,128)} %get-tuple-element.60), channel_id=1, source_target_pairs={{0,4},{4,8},{8,12},{1,5},{5,9},{9,13},{2,6},{6,10},{10,14},{3,7},{... | collective-permute-start | bytes 602120 | tf_op jit(solution)/shard_map/ppermute | solution.py:26
  9.3 0.0 copy-done.18
  9.4 0.0 copy-done.17
  9.4 0.1 add_convert_fusion
  9.5 0.0 copy-done.2
  9.5 0.0 copy-done.7
  9.5 0.0 copy-done.5
  9.5 0.0 copy-start
  9.5 0.0 copy-start.4
  9.5 1.9 %convolution_convert_fusion.refs_7_ = bf16[768,512]{1,0:T(8,128)(2,1)} fusion(bf16[512,512]{1,0:T(8,128)(2,1)S(1)} %copy-done.2, bf16[768,256]{1,0:T(8,128)(2,1)S(1)} %bitcast.20, bf16[256,512]{1,0:T(8,128)(2,1)S(1)} %copy-done.5, f32[512]{0:T(512)S(1)} %copy-done.7), kind=kOutput, calls=%fused_computation.15 | convolution fusion | flops 608305152 | bytes 1968128 | tf_op jit(solution)/shard_map/dot_general | solution.py:618
  11.4 0.0 copy-done
  11.4 0.0 copy-done.4
  11.4 0.1 fusion
  11.5 1.1 collective-permute-done.1
  12.6 1.3 %collective-permute-done = f32[49,8,128]{2,1,0:T(8,128)S(1)} collective-permute-done((f32[49,8,128]{2,1,0:T(8,128)}, f32[49,8,128]{2,1,0:T(8,128)S(1)}, u32[]{:S(2)}, u32[]{:S(2)}) %collective-permute-start) | collective-permute-done | bytes 200736 | tf_op jit(solution)/shard_map/ppermute | solution.py:26
  13.9 1.4 %pack_columns.1 = (f32[5,56,128]{2,1,0:T(8,128)S(1)}, f32[5,56,128]{2,1,0:T(8,128)S(1)}) custom-call(f32[3072,128]{1,0:T(8,128)S(1)} %bitcast.16, f32[64,128]{1,0:T(8,128)S(1)} %copy-done.4, f32[392,128]{1,0:T(8,128)S(1)} %bitcast.26, f32[392,128]{1,0:T(8,128)S(1)} %bitcast.22), custom_call_target="tpu_custom_call" | custom-call | tf_op jit(solution)/shard_map/pack_columns/pallas_call | solution.py:551
  15.4 0.1 pad_maximum_fusion.1
  15.5 0.0 copy-start.3
  15.5 0.3 constant_dynamic-slice_fusion
  15.8 0.0 copy-start.8
  15.8 0.0 copy-start.9
  15.8 0.0 copy-start.15
  15.8 4.0 %collective-permute-start.5 = (f32[5,56,128]{2,1,0:T(8,128)S(1)}, f32[5,56,128]{2,1,0:T(8,128)S(1)}, u32[]{:S(2)}, u32[]{:S(2)}) collective-permute-start(f32[5,56,128]{2,1,0:T(8,128)S(1)} %get-tuple-element.39), channel_id=1, source_target_pairs={{0,1},{1,2},{2,3},{4,5},{5,6},{6,7},{8,9},{9,10},{10,11},{12,13},{... | collective-permute-start | bytes 430088 | tf_op jit(solution)/shard_map/ppermute | solution.py:26
  19.8 1.3 %collective-permute-start.6 = (f32[5,56,128]{2,1,0:T(8,128)S(1)}, f32[5,56,128]{2,1,0:T(8,128)S(1)}, u32[]{:S(2)}, u32[]{:S(2)}) collective-permute-start(f32[5,56,128]{2,1,0:T(8,128)S(1)} %get-tuple-element.40), channel_id=1, source_target_pairs={{1,0},{2,1},{3,2},{5,4},{6,5},{7,6},{9,8},{10,9},{11,10},{13,12},{... | collective-permute-start | bytes 430088 | tf_op jit(solution)/shard_map/ppermute | solution.py:26
  21.1 2.7 %collective-permute-start.2 = (bf16[49,32,128]{2,1,0:T(8,128)(2,1)S(1)}, bf16[49,32,128]{2,1,0:T(8,128)(2,1)S(1)}, u32[]{:S(2)}, u32[]{:S(2)}) collective-permute-start(bf16[49,32,128]{2,1,0:T(8,128)(2,1)S(1)} %get-tuple-element.35), channel_id=1, source_target_pairs={{0,1},{1,2},{2,3},{3,0},{4,5},{5,6},{6,7},{7,4},{8,9},{9,10},{10,1... | collective-permute-start | bytes 1204232 | tf_op jit(solution)/shard_map/ppermute | solution.py:565
  23.8 2.6 %collective-permute-start.3 = (bf16[49,32,128]{2,1,0:T(8,128)(2,1)S(1)}, bf16[49,32,128]{2,1,0:T(8,128)(2,1)S(1)}, u32[]{:S(2)}, u32[]{:S(2)}) collective-permute-start(bf16[49,32,128]{2,1,0:T(8,128)(2,1)S(1)} %get-tuple-element.36), channel_id=1, source_target_pairs={{0,2},{1,3},{2,0},{3,1},{4,6},{5,7},{6,4},{7,5},{8,10},{9,11},{10,... | collective-permute-start | bytes 1204232 | tf_op jit(solution)/shard_map/ppermute | solution.py:565
  26.4 1.3 %collective-permute-start.4 = (bf16[49,32,128]{2,1,0:T(8,128)(2,1)S(1)}, bf16[49,32,128]{2,1,0:T(8,128)(2,1)S(1)}, u32[]{:S(2)}, u32[]{:S(2)}) collective-permute-start(bf16[49,32,128]{2,1,0:T(8,128)(2,1)S(1)} %get-tuple-element.37), channel_id=1, source_target_pairs={{0,3},{1,0},{2,1},{3,2},{4,7},{5,4},{6,5},{7,6},{8,11},{9,8},{10,9... | collective-permute-start | bytes 1204232 | tf_op jit(solution)/shard_map/ppermute | solution.py:565
  27.7 0.0 copy-done.10
  27.7 0.0 copy-done.3
  27.7 11.0 %decoder_order.1.refs_8_ = bf16[512,8192]{1,0:T(8,128)(2,1)S(1)} custom-call(bf16[512,16,512]{2,1,0:T(8,128)(2,1)S(1)} %copy-done.10, bf16[512,512]{1,0:T(8,128)(2,1)S(1)} %copy-done.3), custom_call_target="tpu_custom_call" | custom-call | flops 10000000000 | bytes 10000000 | tf_op jit(solution)/shard_map/decoder_order/pallas_call | solution.py:568
  38.7 0.0 collective-permute-done.5.refs_4_
  38.7 0.0 copy-start.11
  38.7 0.0 collective-permute-done.6.refs_5_
  38.7 0.0 copy-done.8
  38.8 0.0 copy-done.9
  38.8 0.0 copy-done.15
  38.8 0.0 copy-start.13
  38.8 9.1 %tile_solver.3.refs_9_ = f32[3072,128]{1,0:T(8,128)} custom-call(f32[3072,128]{1,0:T(8,128)S(1)} %bitcast.17, f32[64,128]{1,0:T(8,128)S(1)} %copy-done.4, f32[392,128]{1,0:T(8,128)S(1)} %bitcast.27, f32[392,128]{1,0:T(8,128)S(1)} %bitcast.23, f32[5,56,128]{2,1,0:T(8,128)S(1)} %collective-permute-done.5.refs_4_, ...), custom_call_target="tpu_custom_call" | custom-call | flops 99999997952 | bytes 10000000 | tf_op jit(solution)/shard_map/tile_solver/pallas_call | solution.py:585
  47.9 0.0 copy-done.13
  47.9 9.1 %tile_solver.4.refs_9_ = f32[3072,128]{1,0:T(8,128)} custom-call(f32[3072,128]{1,0:T(8,128)S(1)} %bitcast.18, f32[64,128]{1,0:T(8,128)S(1)} %copy-done.4, f32[392,128]{1,0:T(8,128)S(1)} %bitcast.28, f32[392,128]{1,0:T(8,128)S(1)} %bitcast.24, f32[5,56,128]{2,1,0:T(8,128)S(1)} %collective-permute-done.5.refs_4_, ...), custom_call_target="tpu_custom_call", output_to_operand_aliasing={{}: (9, {})} | custom-call | flops 10000000000 | bytes 10000000 | tf_op jit(solution)/shard_map/tile_solver/pallas_call | solution.py:585
  57.1 0.0 collective-permute-done.2.refs_1_
  57.1 0.0 collective-permute-done.3.refs_2_
  57.1 0.0 collective-permute-done.4.refs_3_
  57.1 0.0 copy-done.1
  57.1 21.6 %strip_solver.1 = (bf16[384,512]{1,0:T(8,128)(2,1)S(1)}, f32[1,512]{1,0:T(1,128)S(1)}) custom-call(bf16[49,32,128]{2,1,0:T(8,128)(2,1)S(1)} %get-tuple-element.34.refs_0_, bf16[49,32,128]{2,1,0:T(8,128)(2,1)S(1)} %collective-permute-done.2.refs_1_, bf16[49,32,128]{2,1,0:T(8,128)(2,1)S(1)} %collective-permute-done.3.refs_2_, ...), custom_call_target="tpu_custom_call" | custom-call | tf_op jit(solution)/shard_map/strip_solver/pallas_call | solution.py:620
  78.7 24.0 %all_to_all.10.pieces_ref = bf16[16,24,512]{2,1,0:T(8,128)(2,1)S(1)} all-to-all(bf16[16,24,512]{2,1,0:T(8,128)(2,1)S(1)} %bitcast.30), channel_id=1, replica_groups=mesh['run'=2,'row'=4,'col'=4] {'row','col'}, dimensions={0} | all-to-all | bytes 786432 | tf_op jit(solution)/shard_map/all_to_all | solution.py:649
  102.7 0.9 share_sum.1
  103.5 3.8 %all-to-all-start.1 = ((bf16[16,32,512]{2,1,0:T(8,128)(2,1)}), bf16[16,32,512]{2,1,0:T(8,128)(2,1)S(1)}, u32[]{:S(2)}, u32[]{:S(2)}) async-start(bf16[16,32,512]{2,1,0:T(8,128)(2,1)} %share_sum.1), calls=%async_computation.1 | async-start | bytes 1048576 | tf_op jit(solution)/shard_map/all_to_all | solution.py:666
  107.4 0.9 copy-done.12
  108.3 0.9 copy-done.14
  109.2 2.0 %copy-done.16 = bf16[1536,1152]{1,0:T(8,128)(2,1)S(1)} copy-done((bf16[1536,1152]{1,0:T(8,128)(2,1)S(1)}, bf16[1536,1152]{1,0:T(8,128)(2,1)}, u32[]{:S(2)}) %copy-start.16) | copy-done | bytes 3538968
  111.2 9.1 %tile_solver.5 = f32[3072,128]{1,0:T(8,128)} custom-call(f32[3072,128]{1,0:T(8,128)S(1)} %bitcast.19, f32[64,128]{1,0:T(8,128)S(1)} %copy-done.4, f32[392,128]{1,0:T(8,128)S(1)} %bitcast.29, f32[392,128]{1,0:T(8,128)S(1)} %bitcast.25, f32[5,56,128]{2,1,0:T(8,128)S(1)} %copy-done.12, f32[5,56,128]{2,1,0:T(8,128)S(1)} %copy-done.14, ...), custom_call_target="tpu_custom_call", output_to_operand_aliasing={{}: (9, {})} | custom-call | flops 10000000000 | bytes 10000000 | tf_op jit(solution)/shard_map/tile_solver/pallas_call | solution.py:585
  120.4 0.0 all-to-all-done.1.mine_ref
  120.4 0.0 collective-permute-start.7
  120.4 1.9 %collective-permute-done.7.other_ref = bf16[16,32,512]{2,1,0:T(8,128)(2,1)S(1)} collective-permute-done((bf16[16,32,512]{2,1,0:T(8,128)(2,1)S(1)}, bf16[16,32,512]{2,1,0:T(8,128)(2,1)S(1)}, u32[]{:S(2)}, u32[]{:S(2)}) %collective-permute-start.7) | collective-permute-done | bytes 524320 | tf_op jit(solution)/shard_map/ppermute | solution.py:669
  122.3 0.9 copy-done.6
  123.2 3.1 %trunk_update.1 = (f32[256,512]{1,0:T(8,128)}, f32[1,512]{1,0:T(1,128)}, f32[512,512]{1,0:T(8,128)}, f32[1,128]{1,0:T(1,128)}) custom-call(bf16[16,32,512]{2,1,0:T(8,128)(2,1)S(1)} %all-to-all-done.1.mine_ref, bf16[16,32,512]{2,1,0:T(8,128)(2,1)S(1)} %collective-permute-done.7.other_ref, bf16[768,256]{1,0:T(8,128)(2,1)S(1)} %bitcast.21, ...), custom_call_target="tpu_custom_call" | custom-call | tf_op jit(solution)/shard_map/trunk_update/pallas_call | solution.py:671
  (11 shorter events, 0.1 us)
Async XLA Ops:
  0.6 8.7 %copy-start.18 = (bf16[8,256]{1,0:T(8,128)(2,1)S(1)}, bf16[8,256]{1,0:T(8,128)(2,1)}, u32[]{:S(2)}) copy-start(bf16[8,256]{1,0:T(8,128)(2,1)} %param.17) | copy-start | bytes 12292
  0.6 8.7 %copy-start.17 = (bf16[96,256]{1,0:T(8,128)(2,1)S(1)}, bf16[96,256]{1,0:T(8,128)(2,1)}, u32[]{:S(2)}) copy-start(bf16[96,256]{1,0:T(8,128)(2,1)} %param.16) | copy-start | bytes 147460
  0.7 8.8 %copy-start.2 = (bf16[512,512]{1,0:T(8,128)(2,1)S(1)}, bf16[512,512]{1,0:T(8,128)(2,1)}, u32[]{:S(2)}) copy-start(bf16[512,512]{1,0:T(8,128)(2,1)} %w_out_ref.1) | copy-start | bytes 1572868
  0.7 8.8 %copy-start.7 = (f32[512]{0:T(512)S(1)}, f32[512]{0:T(512)}, u32[]{:S(2)}) copy-start(f32[512]{0:T(512)} %param.19) | copy-start | bytes 6148
  0.7 8.8 %copy-start.5 = (bf16[256,512]{1,0:T(8,128)(2,1)S(1)}, bf16[256,512]{1,0:T(8,128)(2,1)}, u32[]{:S(2)}) copy-start(bf16[256,512]{1,0:T(8,128)(2,1)} %w_in_ref.1) | copy-start | bytes 786436
  2.6 10.0 %collective-permute-start.1 = (f32[49,8,128]{2,1,0:T(8,128)}, f32[49,8,128]{2,1,0:T(8,128)S(1)}, u32[]{:S(2)}, u32[]{:S(2)}) collective-permute-start(f32[49,8,128]{2,1,0:T(8,128)} %get-tuple-element.59), channel_id=1, source_target_pairs={{4,0},{8,4},{12,8},{5,1},{9,5},{13,9},{6,2},{10,6},{14,10},{7,3},{... | collective-permute-start | bytes 602120 | tf_op jit(solution)/shard_map/ppermute | solution.py:26
  3.8 10.0 %collective-permute-start = (f32[49,8,128]{2,1,0:T(8,128)}, f32[49,8,128]{2,1,0:T(8,128)S(1)}, u32[]{:S(2)}, u32[]{:S(2)}) collective-permute-start(f32[49,8,128]{2,1,0:T(8,128)} %get-tuple-element.60), channel_id=1, source_target_pairs={{0,4},{4,8},{8,12},{1,5},{5,9},{9,13},{2,6},{6,10},{10,14},{3,7},{... | collective-permute-start | bytes 602120 | tf_op jit(solution)/shard_map/ppermute | solution.py:26
  9.5 1.9 %copy-start = (f32[48,64,128]{2,1,0:T(8,128)S(1)}, f32[48,64,128]{2,1,0:T(8,128)}, u32[]{:S(2)}) copy-start(f32[48,64,128]{2,1,0:T(8,128)} %param.12) | copy-start | bytes 4718596
  9.5 1.9 %copy-start.4 = (f32[64,128]{1,0:T(8,128)S(1)}, f32[64,128]{1,0:T(8,128)}, u32[]{:S(2)}) copy-start(f32[64,128]{1,0:T(8,128)} %refs_1_.5) | copy-start | bytes 98308
  11.4 16.3 %copy-start.10 = (bf16[512,16,512]{2,1,0:T(8,128)(2,1)S(1)}, bf16[512,16,512]{2,1,0:T(8,128)(2,1)}, u32[]{:S(2)}) copy-start(bf16[512,16,512]{2,1,0:T(8,128)(2,1)} %d_ref.1) | copy-start | bytes 25165828
  15.5 12.3 %copy-start.3 = (bf16[512,512]{1,0:T(8,128)(2,1)S(1)}, bf16[512,512]{1,0:T(8,128)(2,1)}, u32[]{:S(2)}) copy-start(bf16[512,512]{1,0:T(8,128)(2,1)} %constant.51.clone.order_ref.refs_4_) | copy-start | bytes 1572868
  15.8 23.0 %copy-start.8 = (f32[48]{0:T(128)S(1)}, f32[48]{0:T(128)}, u32[]{:S(2)}) copy-start(f32[48]{0:T(128)} %refs_6_.7) | copy-start | bytes 580
  15.8 23.0 %copy-start.9 = (s32[48]{0:T(128)S(1)}, s32[48]{0:T(128)}, u32[]{:S(2)}) copy-start(s32[48]{0:T(128)} %refs_7_.5) | copy-start | bytes 580
  15.8 23.0 %copy-start.15 = (bf16[1536,1152]{1,0:T(8,128)(2,1)S(1)}, bf16[1536,1152]{1,0:T(8,128)(2,1)}, u32[]{:S(2)}) copy-start(bf16[1536,1152]{1,0:T(8,128)(2,1)} %constant.52.clone.refs_8_) | copy-start | bytes 10616836
  15.8 22.9 %collective-permute-start.5 = (f32[5,56,128]{2,1,0:T(8,128)S(1)}, f32[5,56,128]{2,1,0:T(8,128)S(1)}, u32[]{:S(2)}, u32[]{:S(2)}) collective-permute-start(f32[5,56,128]{2,1,0:T(8,128)S(1)} %get-tuple-element.39), channel_id=1, source_target_pairs={{0,1},{1,2},{2,3},{4,5},{5,6},{6,7},{8,9},{9,10},{10,11},{12,13},{... | collective-permute-start | bytes 430088 | tf_op jit(solution)/shard_map/ppermute | solution.py:26
  19.8 18.9 %collective-permute-start.6 = (f32[5,56,128]{2,1,0:T(8,128)S(1)}, f32[5,56,128]{2,1,0:T(8,128)S(1)}, u32[]{:S(2)}, u32[]{:S(2)}) collective-permute-start(f32[5,56,128]{2,1,0:T(8,128)S(1)} %get-tuple-element.40), channel_id=1, source_target_pairs={{1,0},{2,1},{3,2},{5,4},{6,5},{7,6},{9,8},{10,9},{11,10},{13,12},{... | collective-permute-start | bytes 430088 | tf_op jit(solution)/shard_map/ppermute | solution.py:26
  21.1 36.0 %collective-permute-start.2 = (bf16[49,32,128]{2,1,0:T(8,128)(2,1)S(1)}, bf16[49,32,128]{2,1,0:T(8,128)(2,1)S(1)}, u32[]{:S(2)}, u32[]{:S(2)}) collective-permute-start(bf16[49,32,128]{2,1,0:T(8,128)(2,1)S(1)} %get-tuple-element.35), channel_id=1, source_target_pairs={{0,1},{1,2},{2,3},{3,0},{4,5},{5,6},{6,7},{7,4},{8,9},{9,10},{10,1... | collective-permute-start | bytes 1204232 | tf_op jit(solution)/shard_map/ppermute | solution.py:565
  23.8 33.3 %collective-permute-start.3 = (bf16[49,32,128]{2,1,0:T(8,128)(2,1)S(1)}, bf16[49,32,128]{2,1,0:T(8,128)(2,1)S(1)}, u32[]{:S(2)}, u32[]{:S(2)}) collective-permute-start(bf16[49,32,128]{2,1,0:T(8,128)(2,1)S(1)} %get-tuple-element.36), channel_id=1, source_target_pairs={{0,2},{1,3},{2,0},{3,1},{4,6},{5,7},{6,4},{7,5},{8,10},{9,11},{10,... | collective-permute-start | bytes 1204232 | tf_op jit(solution)/shard_map/ppermute | solution.py:565
  26.4 30.7 %collective-permute-start.4 = (bf16[49,32,128]{2,1,0:T(8,128)(2,1)S(1)}, bf16[49,32,128]{2,1,0:T(8,128)(2,1)S(1)}, u32[]{:S(2)}, u32[]{:S(2)}) collective-permute-start(bf16[49,32,128]{2,1,0:T(8,128)(2,1)S(1)} %get-tuple-element.37), channel_id=1, source_target_pairs={{0,3},{1,0},{2,1},{3,2},{4,7},{5,4},{6,5},{7,6},{8,11},{9,8},{10,9... | collective-permute-start | bytes 1204232 | tf_op jit(solution)/shard_map/ppermute | solution.py:565
  38.7 9.2 %copy-start.11 = (f32[5,56,128]{2,1,0:T(8,128)}, f32[5,56,128]{2,1,0:T(8,128)S(1)}, u32[]{:S(2)}) copy-start(f32[5,56,128]{2,1,0:T(8,128)S(1)} %collective-permute-done.5.refs_4_) | copy-start | bytes 430084
  38.8 9.2 %copy-start.13 = (f32[5,56,128]{2,1,0:T(8,128)}, f32[5,56,128]{2,1,0:T(8,128)S(1)}, u32[]{:S(2)}) copy-start(f32[5,56,128]{2,1,0:T(8,128)S(1)} %collective-permute-done.6.refs_5_) | copy-start | bytes 430084
  47.9 9.2 %copy-start.1 = (bf16[768,512]{1,0:T(8,128)(2,1)S(1)}, bf16[768,512]{1,0:T(8,128)(2,1)}, u32[]{:S(2)}) copy-start(bf16[768,512]{1,0:T(8,128)(2,1)} %convolution_convert_fusion.refs_7_) | copy-start | bytes 2359300
  103.5 16.8 %all-to-all-start.1 = ((bf16[16,32,512]{2,1,0:T(8,128)(2,1)}), bf16[16,32,512]{2,1,0:T(8,128)(2,1)S(1)}, u32[]{:S(2)}, u32[]{:S(2)}) async-start(bf16[16,32,512]{2,1,0:T(8,128)(2,1)} %share_sum.1), calls=%async_computation.1 | async-start | bytes 1048576 | tf_op jit(solution)/shard_map/all_to_all | solution.py:666
  107.4 0.9 copy-start.12
  108.3 0.9 copy-start.14
  109.2 2.0 %copy-start.16 = (bf16[1536,1152]{1,0:T(8,128)(2,1)S(1)}, bf16[1536,1152]{1,0:T(8,128)(2,1)}, u32[]{:S(2)}) copy-start(bf16[1536,1152]{1,0:T(8,128)(2,1)} %constant.52.clone.refs_8_) | copy-start | bytes 10616836
  120.4 1.9 %collective-permute-start.7 = (bf16[16,32,512]{2,1,0:T(8,128)(2,1)S(1)}, bf16[16,32,512]{2,1,0:T(8,128)(2,1)S(1)}, u32[]{:S(2)}, u32[]{:S(2)}) collective-permute-start(bf16[16,32,512]{2,1,0:T(8,128)(2,1)S(1)} %all-to-all-done.1.mine_ref), channel_id=1, source_target_pairs={{0,16},{16,0},{1,17},{17,1},{2,18},{18,2},{3,19},{19,3},{4,20},{20... | collective-permute-start | bytes 1572872 | tf_op jit(solution)/shard_map/ppermute | solution.py:669
  122.3 1.0 copy-start.6
